TPU v7x, 256 devices: a whole 4x4x8 slice. The times are simulated.
256 devices in a mesh: expert: 32 (over z, y), tensor: 8 (over x, core).
Axes of the slice: x: 4, y: 4, z: 8, core: 2. Of those that a mesh axis runs over, the one named last changes fastest.
Arguments:
- tokens: bfloat16 [2048, 5120], P(('expert', 'tensor')), may hold values from -6 to 6
- routes: int32 [2048, 6], P(('expert', 'tensor')), may hold values from 0 to 31, all different within a row; in each aligned block of 64 rows (0 to 63, 64 to 127, ...) at most 16 rows name the same one
- gate_num: int32 [2048, 6], P(('expert', 'tensor')), may hold values from 1 to 64
- cotangent: bfloat16 [2048, 5120], P(('expert', 'tensor')), may hold values from -6 to 6
- w_in: bfloat16 [32, 2, 768, 5120], P('expert', None, 'tensor'), may hold values from -0.078125 to 0.078125
- w_out: bfloat16 [32, 768, 5120], P('expert', 'tensor'), may hold values from -0.21875 to 0.21875
- shared_in: bfloat16 [2, 1536, 5120], P(None, 'tensor'), may hold values from -0.078125 to 0.078125
- shared_out: bfloat16 [1536, 5120], P('tensor'), may hold values from -0.15625 to 0.15625
Outputs:
- output: bfloat16 [2048, 5120], P(('expert', 'tensor'))
- grad_tokens: bfloat16 [2048, 5120], P(('expert', 'tensor'))
- grad_in: bfloat16 [32, 2, 768, 5120], P('expert', None, 'tensor')
- grad_out: bfloat16 [32, 768, 5120], P('expert', 'tensor')
Inputs may be any that keep to these rules, and one draw needn't show every extreme that they name: `routes`: each row names 6 different experts. In each group of 64 tokens no expert is named by more than 16 tokens, a bound that some block reaches.
All inputs are finite; a program needn't handle non-finite values.
Results may differ from a plain program's by a relative error of at most 0.019.
Values may be sent and summed in bfloat16 or wider, within the bound.
A program may use at most 128 MiB of HBM per device.

v0:
```python
import jax
import jax.numpy as jnp
from jax import lax
from jax.sharding import PartitionSpec as P

TOPK = 6


denominator = 64.0


def silu_parts(preact):
    sig_value = jax.nn.sigmoid(preact)
    return (preact * sig_value, sig_value * (1.0 + preact * (1.0 - sig_value)))


def slot_tables(route_rows, gate_rows, experts, capacity):
    row_count, top_count = route_rows.shape
    flat_ids = route_rows.reshape(row_count * top_count)
    expert_ids = jnp.arange(experts, dtype=jnp.int32)
    onehot = (flat_ids[:, None] == expert_ids[None, :]).astype(jnp.int32)
    before = jnp.cumsum(onehot, axis=0, dtype=jnp.int32) - onehot
    slot_rank = jnp.sum(before * onehot, axis=1, dtype=jnp.int32)
    slot_index = (flat_ids * capacity + slot_rank).reshape(row_count, top_count)
    positions = jnp.arange(experts * capacity, dtype=jnp.int32)
    matches = slot_index[None, :, :] == positions[:, None, None]
    select = jnp.sum(jnp.where(matches, jnp.float32(1.0), jnp.float32(0.0)), axis=2)
    gate_share = gate_rows.astype(jnp.float32) / denominator
    weight = jnp.sum(jnp.where(matches, gate_share[None, :, :], jnp.float32(0.0)), axis=2)
    return (select, weight)


def contract_rows(left, right, precision=None):
    return lax.dot_general(
        left,
        right,
        (((0,), (0,)), ((), ())),
        precision=precision,
        preferred_element_type=jnp.float32,
    )


def contract_last(left, right):
    return lax.dot_general(
        left, right, (((1,), (1,)), ((), ())), preferred_element_type=jnp.float32
    )


def on_device(tokens, routes, gate_num, cotangent, w_in, w_out, shared_in, shared_out):
    experts = lax.axis_size("expert")
    group_x, group_dy = (
        lax.all_gather(tokens, "tensor", axis=0, tiled=True),
        lax.all_gather(cotangent, "tensor", axis=0, tiled=True),
    )
    group_routes, group_gates = (
        lax.all_gather(routes, "tensor", axis=0, tiled=True),
        lax.all_gather(gate_num, "tensor", axis=0, tiled=True),
    )
    row_count = group_x.shape[0]
    features = group_x.shape[1]
    capacity = 4 * row_count * TOPK // (3 * experts)
    select, weight = slot_tables(group_routes, group_gates, experts, capacity)
    select_half = select.astype(jnp.bfloat16)
    weight_half = weight.astype(jnp.bfloat16)
    send_x = jnp.dot(select_half, group_x, preferred_element_type=jnp.float32).astype(jnp.bfloat16)
    send_x = send_x.reshape(experts, capacity, features)
    send_dy = jnp.dot(weight_half, group_dy, preferred_element_type=jnp.float32).astype(
        jnp.bfloat16
    )
    send_dy = send_dy.reshape(experts, capacity, features)
    got_x, got_dy = (
        lax.all_to_all(send_x, "expert", split_axis=0, concat_axis=0, tiled=True),
        lax.all_to_all(send_dy, "expert", split_axis=0, concat_axis=0, tiled=True),
    )
    flat_x = got_x.reshape(experts * capacity, features)
    flat_dy = got_dy.reshape(experts * capacity, features)
    gate_pre = contract_last(flat_x, w_in[0, 0])
    up_pre = contract_last(flat_x, w_in[0, 1])
    active, slopes = silu_parts(gate_pre)
    hidden = (active * up_pre).astype(jnp.bfloat16)
    out_part = jnp.dot(hidden, w_out[0], preferred_element_type=jnp.float32).astype(jnp.bfloat16)
    back_grad = contract_last(flat_dy, w_out[0])
    d_gate = (back_grad * up_pre * slopes).astype(jnp.bfloat16)
    d_up = (back_grad * active).astype(jnp.bfloat16)
    x_part = (
        jnp.dot(d_gate, w_in[0, 0], preferred_element_type=jnp.float32)
        + jnp.dot(d_up, w_in[0, 1], preferred_element_type=jnp.float32)
    ).astype(jnp.bfloat16)
    grad_out = contract_rows(hidden, flat_dy).astype(jnp.bfloat16)[None]
    grad_in = jnp.stack([contract_rows(d_gate, flat_x), contract_rows(d_up, flat_x)]).astype(
        jnp.bfloat16
    )[None]
    out_part = out_part.reshape(experts, capacity, features)
    x_part = x_part.reshape(experts, capacity, features)
    back_out, back_x = (
        lax.all_to_all(out_part, "expert", split_axis=0, concat_axis=0, tiled=True),
        lax.all_to_all(x_part, "expert", split_axis=0, concat_axis=0, tiled=True),
    )
    routed_y = contract_rows(weight_half, back_out.reshape(experts * capacity, features))
    routed_dx = contract_rows(select_half, back_x.reshape(experts * capacity, features))
    shared_gate = contract_last(group_x, shared_in[0])
    shared_up = contract_last(group_x, shared_in[1])
    shared_act, shared_slope = silu_parts(shared_gate)
    shared_hidden = (shared_act * shared_up).astype(jnp.bfloat16)
    shared_y = jnp.dot(shared_hidden, shared_out, preferred_element_type=jnp.float32)
    shared_back = contract_last(group_dy, shared_out)
    shared_dgate = (shared_back * shared_up * shared_slope).astype(jnp.bfloat16)
    shared_dup = (shared_back * shared_act).astype(jnp.bfloat16)
    shared_dx = jnp.dot(shared_dgate, shared_in[0], preferred_element_type=jnp.float32) + jnp.dot(
        shared_dup, shared_in[1], preferred_element_type=jnp.float32
    )
    output, grad_tokens = (
        lax.psum_scatter(
            (shared_y + routed_y).astype(jnp.bfloat16), "tensor", scatter_dimension=0, tiled=True
        ).astype(jnp.float32),
        lax.psum_scatter(
            (shared_dx + routed_dx).astype(jnp.bfloat16), "tensor", scatter_dimension=0, tiled=True
        ).astype(jnp.float32),
    )
    return (output.astype(jnp.bfloat16), grad_tokens.astype(jnp.bfloat16), grad_in, grad_out)


def solution(mesh):
    in_specs = (
        P(("expert", "tensor"), None),
        P(("expert", "tensor"), None),
        P(("expert", "tensor"), None),
        P(("expert", "tensor"), None),
        P("expert", None, "tensor", None),
        P("expert", "tensor", None),
        P(None, "tensor", None),
        P("tensor", None),
    )
    out_specs = (
        P(("expert", "tensor"), None),
        P(("expert", "tensor"), None),
        P("expert", None, "tensor", None),
        P("expert", "tensor", None),
    )
    return jax.shard_map(
        on_device, mesh=mesh, in_specs=in_specs, out_specs=out_specs, check_vma=False
    )
```

profile of v0, /device:TPU:1, one launch (start us, length us, event | category | flops | bytes accessed | tf_op | source)
XLA Modules:
  0.0 614.4 jit_solution(1283523525614283220)
XLA Ops:
  7.2 16.1 %all_gather.13 = s32[64,6]{1,0:T(8,128)S(1)} all-gather(s32[8,6]{1,0:T(8,128)} %param.9), channel_id=1, replica_groups=mesh['expert'=32,'tensor'=8] {'tensor'}, dimensions={0}, use_global_device_ids=true | all-gather | bytes 1728 | tf_op jit(solution)/shard_map/all_gather | solution.py:56
  23.6 13.0 %all_gather.14 = s32[64,6]{1,0:T(8,128)S(1)} all-gather(s32[8,6]{1,0:T(8,128)} %param.10), channel_id=1, replica_groups=mesh['expert'=32,'tensor'=8] {'tensor'}, dimensions={0}, use_global_device_ids=true | all-gather | bytes 1728 | tf_op jit(solution)/shard_map/all_gather | solution.py:57
  38.1 13.5 %all_gather.12 = bf16[64,5120]{1,0:T(8,128)(2,1)S(1)} all-gather(bf16[8,5120]{1,0:T(8,128)(2,1)} %param.8), channel_id=1, replica_groups=mesh['expert'=32,'tensor'=8] {'tensor'}, dimensions={0}, use_global_device_ids=true | all-gather | bytes 737280 | tf_op jit(solution)/shard_map/all_gather | solution.py:52
  51.8 3.9 convolution_convert_fusion.2
  55.7 10.1 %all-to-all-start = ((bf16[32,16,5120]{2,1,0:T(8,128)(2,1)}), bf16[32,16,5120]{2,1,0:T(8,128)(2,1)}, u32[]{:S(2)}, u32[]{:S(2)}) async-start(bf16[32,16,5120]{2,1,0:T(8,128)(2,1)} %bitcast.88), calls=%async_computation | async-start | bytes 10485760 | tf_op jit(solution)/shard_map/all_to_all | solution.py:72
  65.8 13.5 %all_gather.15 = bf16[64,5120]{1,0:T(8,128)(2,1)S(1)} all-gather(bf16[8,5120]{1,0:T(8,128)(2,1)S(1)} %copy-done.12), channel_id=1, replica_groups=mesh['expert'=32,'tensor'=8] {'tensor'}, dimensions={0}, use_global_device_ids=true | all-gather | bytes 737280 | tf_op jit(solution)/shard_map/all_gather | solution.py:53
  79.3 3.9 convolution_convert_fusion
  83.2 101.8 %all-to-all-done = bf16[32,16,5120]{2,1,0:T(8,128)(2,1)} async-done(((bf16[32,16,5120]{2,1,0:T(8,128)(2,1)}), bf16[32,16,5120]{2,1,0:T(8,128)(2,1)}, u32[]{:S(2)}, u32[]{:S(2)}) %all-to-all-start) | async-done | bytes 5242912 | tf_op jit(solution)/shard_map/all_to_all | solution.py:72
  185.0 7.9 %all-to-all-start.2 = ((bf16[32,16,5120]{2,1,0:T(8,128)(2,1)}), bf16[32,16,5120]{2,1,0:T(8,128)(2,1)}, u32[]{:S(2)}, u32[]{:S(2)}) async-start(bf16[32,16,5120]{2,1,0:T(8,128)(2,1)} %bitcast.86), calls=%async_computation.3 | async-start | bytes 10485760 | tf_op jit(solution)/shard_map/all_to_all | solution.py:73
  192.9 5.3 fusion.21
  198.2 4.9 fusion.25
  203.1 104.2 %all-to-all-done.2 = bf16[32,16,5120]{2,1,0:T(8,128)(2,1)} async-done(((bf16[32,16,5120]{2,1,0:T(8,128)(2,1)}), bf16[32,16,5120]{2,1,0:T(8,128)(2,1)}, u32[]{:S(2)}, u32[]{:S(2)}) %all-to-all-start.2) | async-done | bytes 5242912 | tf_op jit(solution)/shard_map/all_to_all | solution.py:73
  307.4 5.3 multiply_convert_fusion
  312.7 3.8 convolution_convert_fusion.1
  316.5 12.4 %all-to-all-start.1 = ((bf16[32,16,5120]{2,1,0:T(8,128)(2,1)}), bf16[32,16,5120]{2,1,0:T(8,128)(2,1)}, u32[]{:S(2)}, u32[]{:S(2)}) async-start(bf16[32,16,5120]{2,1,0:T(8,128)(2,1)} %bitcast.87), calls=%async_computation.1 | async-start | bytes 10485760 | tf_op jit(solution)/shard_map/all_to_all | solution.py:96
  328.9 2.9 fusion.23
  331.8 3.9 add_convert_fusion
  335.8 107.6 %all-to-all-done.1 = bf16[32,16,5120]{2,1,0:T(8,128)(2,1)} async-done(((bf16[32,16,5120]{2,1,0:T(8,128)(2,1)}), bf16[32,16,5120]{2,1,0:T(8,128)(2,1)}, u32[]{:S(2)}, u32[]{:S(2)}) %all-to-all-start.1) | async-done | bytes 5242912 | tf_op jit(solution)/shard_map/all_to_all | solution.py:96
  443.3 11.7 %all-to-all-start.3 = ((bf16[32,16,5120]{2,1,0:T(8,128)(2,1)}), bf16[32,16,5120]{2,1,0:T(8,128)(2,1)}, u32[]{:S(2)}, u32[]{:S(2)}) async-start(bf16[32,16,5120]{2,1,0:T(8,128)(2,1)} %bitcast.89), calls=%async_computation.4 | async-start | bytes 10485760 | tf_op jit(solution)/shard_map/all_to_all | solution.py:97
  455.0 2.3 fusion.11
  457.3 2.3 fusion.7
  459.7 1.4 fusion.49
  461.1 3.5 fusion.51
  466.0 2.1 fusion.9
  468.1 4.4 fusion.5
  472.5 96.5 %all-to-all-done.3 = bf16[32,16,5120]{2,1,0:T(8,128)(2,1)} async-done(((bf16[32,16,5120]{2,1,0:T(8,128)(2,1)}), bf16[32,16,5120]{2,1,0:T(8,128)(2,1)}, u32[]{:S(2)}, u32[]{:S(2)}) %all-to-all-start.3) | async-done | bytes 5242912 | tf_op jit(solution)/shard_map/all_to_all | solution.py:97
  569.0 3.7 fusion.50
  572.7 1.4 fusion.1
  574.1 3.5 fusion.4
  577.7 3.5 fusion.3
  581.1 1.4 pad_maximum_fusion
  582.6 25.0 %reduce-scatter.5.cloned.1.call-done = bf16[8,5120]{1,0:T(8,128)(2,1)} async-done(((bf16[64,5120]{1,0:T(8,128)(2,1)}), bf16[8,5120]{1,0:T(8,128)(2,1)}) %reduce-scatter.5.cloned.1.call-update) | async-done | bytes 81936 | tf_op jit(solution)/shard_map/reduce_scatter | solution.py:116
  (45 shorter events, 3.5 us)
Async XLA Ops:
  7.2 452.5 %copy-start = (bf16[192,5120]{1,0:T(8,128)(2,1)S(1)}, bf16[192,5120]{1,0:T(8,128)(2,1)}, u32[]{:S(2)}) copy-start(bf16[192,5120]{1,0:T(8,128)(2,1)} %param.15) | copy-start | bytes 5898244
  55.7 10.1 %copy-start.12 = (bf16[8,5120]{1,0:T(8,128)(2,1)S(1)}, bf16[8,5120]{1,0:T(8,128)(2,1)}, u32[]{:S(2)}) copy-start(bf16[8,5120]{1,0:T(8,128)(2,1)} %param.11) | copy-start | bytes 245764
  55.7 129.3 %all-to-all-start = ((bf16[32,16,5120]{2,1,0:T(8,128)(2,1)}), bf16[32,16,5120]{2,1,0:T(8,128)(2,1)}, u32[]{:S(2)}, u32[]{:S(2)}) async-start(bf16[32,16,5120]{2,1,0:T(8,128)(2,1)} %bitcast.88), calls=%async_computation | async-start | bytes 10485760 | tf_op jit(solution)/shard_map/all_to_all | solution.py:72
  185.0 122.4 %all-to-all-start.2 = ((bf16[32,16,5120]{2,1,0:T(8,128)(2,1)}), bf16[32,16,5120]{2,1,0:T(8,128)(2,1)}, u32[]{:S(2)}, u32[]{:S(2)}) async-start(bf16[32,16,5120]{2,1,0:T(8,128)(2,1)} %bitcast.86), calls=%async_computation.3 | async-start | bytes 10485760 | tf_op jit(solution)/shard_map/all_to_all | solution.py:73
  192.9 5.3 copy-start.2
  307.4 5.3 copy-start.4
  316.5 126.8 %all-to-all-start.1 = ((bf16[32,16,5120]{2,1,0:T(8,128)(2,1)}), bf16[32,16,5120]{2,1,0:T(8,128)(2,1)}, u32[]{:S(2)}, u32[]{:S(2)}) async-start(bf16[32,16,5120]{2,1,0:T(8,128)(2,1)} %bitcast.87), calls=%async_computation.1 | async-start | bytes 10485760 | tf_op jit(solution)/shard_map/all_to_all | solution.py:96
  328.9 3.0 copy-start.3
  328.9 3.0 copy-start.10
  443.3 125.7 %all-to-all-start.3 = ((bf16[32,16,5120]{2,1,0:T(8,128)(2,1)}), bf16[32,16,5120]{2,1,0:T(8,128)(2,1)}, u32[]{:S(2)}, u32[]{:S(2)}) async-start(bf16[32,16,5120]{2,1,0:T(8,128)(2,1)} %bitcast.89), calls=%async_computation.4 | async-start | bytes 10485760 | tf_op jit(solution)/shard_map/all_to_all | solution.py:97
  455.0 127.6 %reduce-scatter.3.cloned.1.call-start = ((), (), s32[]{:S(2)}) async-start(), calls=%async_computation.6 | async-start | bytes 737280 | tf_op jit(solution)/shard_map/reduce_scatter | solution.py:113
  457.3 7.3 %copy-start.5 = (f32[64,192]{1,0:T(8,128)}, f32[64,192]{1,0:T(8,128)S(1)}, u32[]{:S(2)}) copy-start(f32[64,192]{1,0:T(8,128)S(1)} %fusion.11) | copy-start | bytes 147460
  459.7 4.9 copy-start.11
  464.6 1.4 copy-start.7
  466.0 141.6 %reduce-scatter.5.cloned.1.call-start = ((), (), s32[]{:S(2)}) async-start(), calls=%async_computation.7 | async-start | bytes 737280 | tf_op jit(solution)/shard_map/reduce_scatter | solution.py:116
  472.5 100.1 %copy-start.6 = (f32[64,192]{1,0:T(8,128)S(1)}, f32[64,192]{1,0:T(8,128)}, u32[]{:S(2)}) copy-start(f32[64,192]{1,0:T(8,128)} %copy-done.5) | copy-start | bytes 147460
  472.5 100.1 %copy-start.8 = (f32[64,192]{1,0:T(8,128)S(1)}, f32[64,192]{1,0:T(8,128)}, u32[]{:S(2)}) copy-start(f32[64,192]{1,0:T(8,128)} %fusion.49) | copy-start | bytes 147460
  569.0 3.7 copy-start.1
  574.1 3.6 copy-start.9
Sparse Core Ops, SparseCore 0:
  466.1 33.5 reduce-scatter.2
  574.3 33.2 reduce-scatter.4
where the time goes:
time: 616 us; the launch traced here: 614 us
  waiting for transfers between devices  435 us (71%)
  matrix products  63.4 us (10%)
  blocking collectives  56.1 us (9%)
  starting transfers between devices  42 us (7%)
  between operations  14.3 us (2%)
    all_to_all x1, waiting for transfers between devices, on_device(): lax.all_to_all(out_part, 'expert', split_axis=0, concat_axis=0, tiled=True)  108 us
    all_to_all x1, waiting for transfers between devices, on_device(): lax.all_to_all(send_dy, 'expert', split_axis=0, concat_axis=0, tiled=True)  104 us
    all_to_all x1, waiting for transfers between devices, on_device(): lax.all_to_all(send_x, 'expert', split_axis=0, concat_axis=0, tiled=True)  102 us
    all_to_all x1, waiting for transfers between devices, on_device(): lax.all_to_all(x_part, 'expert', split_axis=0, concat_axis=0, tiled=True)  96.5 us
    reduce_scatter x1, waiting for transfers between devices, on_device(): lax.psum_scatter((shared_dx + routed_dx).astype(jnp.bfloat16), 'tensor',...  25 us
    dot_general x6, matrix products, contract_last(): lax.dot_general(left, right, (((1,), (1,)), ((), ())), preferred_element_...  21.5 us
    dot_general x5, matrix products, contract_rows(): lax.dot_general(left, right, (((0,), (0,)), ((), ())), precision=precisio...  18.6 us
    all_gather x1, blocking collectives, on_device(): lax.all_gather(routes, 'tensor', axis=0, tiled=True)  16.1 us
  transfers between devices with their start and end apart: 6, of which 5 were waited for; matrix products, arithmetic and copies ran while one was open for 8% of the time, Pallas kernels for 0%

commit v1 on v0

v1 whole, which is shorter than its diff:
```python
import functools

import jax
import jax.numpy as jnp
from jax import lax
from jax.experimental import pallas as pl
from jax.experimental.pallas import tpu as pltpu
from jax.sharding import PartitionSpec as P

MESH = pl.DeviceIdType.MESH
BF = jnp.bfloat16
F32 = jnp.float32
SLOTS = 16
NT = (((1,), (1,)), ((), ()))
TN = (((0,), (0,)), ((), ()))

TAB, SLICE, TOKENS, WEIGHT, DISPATCH, PARTNER, PRE, ACT, GRAD_IN, GRAD_OUT, SHARED, FINAL, BACK = range(13)
HALF = 13
COUNT = 17


def dot(left, right, dims=None):
    dims = dims or (((1,), (0,)), ((), ()))
    return lax.dot_general(left, right, dims, preferred_element_type=F32)


def silu_parts(preact):
    sig_value = jax.nn.sigmoid(preact)
    return preact * sig_value, sig_value * (1.0 + preact * (1.0 - sig_value))


def kernel(
    topk,
    pair_ref, table_ref, w_in, w_out, sh_in, sh_out,
    out_ref, gtok_ref, gin_ref, gout_ref,
    tabs, gs, g, wt, sw_in, sw_out, t2, snd, xr, pf, pb, rs, act, ps, pr, ret, bk, gb, shs, shr, fs, fr,
    ssem, rsem, lsem,
):
    ne, nt = lax.axis_size("expert"), lax.axis_size("tensor")
    e, t = lax.axis_index("expert"), lax.axis_index("tensor")
    chip, core = t // 2, t % 2
    chips = nt // 2
    d8 = gs.shape[1]
    hid = w_out.shape[0]
    half = chips * hid
    gc = ne // chips
    rows = gc * SLOTS
    m32 = 2 * SLOTS

    def rcopy(src, dst, which, dev):
        return pltpu.make_async_remote_copy(
            src_ref=src, dst_ref=dst, send_sem=ssem.at[which], recv_sem=rsem.at[which],
            device_id=dev, device_id_type=MESH,
        )

    def recv(ref, which):
        pltpu.make_async_copy(ref, ref, rsem.at[which]).wait()

    def sent(ref, which):
        pltpu.make_async_copy(ref, ref, ssem.at[which]).wait()

    def cols(piece):
        return pl.ds(pl.multiple_of(piece * d8, 128), d8)

    def block(index, size):
        return pl.ds(pl.multiple_of(index * size, 16), size)

    own_shared = [
        pltpu.make_async_copy(sh_in, sw_in, lsem.at[0]),
        pltpu.make_async_copy(sh_out, sw_out, lsem.at[1]),
    ]
    own_weights = []
    for h in range(2):
        for m in range(3):
            source = w_out if m == 2 else w_in.at[m]
            own_weights.append(pltpu.make_async_copy(
                source.at[:, cols(2 * chip + h)], wt.at[h, m, block(chip, hid)], lsem.at[2 + 3 * h + m]))
    for copy in own_weights + own_shared:
        copy.start()

    barrier = pltpu.get_barrier_semaphore()

    @pl.loop(1, ne)
    def _(k):
        pl.semaphore_signal(barrier, inc=1, device_id=(lax.rem(e + k, ne), t), device_id_type=MESH)

    @pl.loop(1, nt)
    def _(k):
        pl.semaphore_signal(barrier, inc=1, device_id=(e, lax.rem(t + k, nt)), device_id_type=MESH)

    pl.semaphore_wait(barrier, ne + nt - 2)

    @pl.loop(1, nt)
    def _(k):
        p = lax.rem(t + k, nt)
        rcopy(table_ref, tabs.at[block(t, 16)], TAB, (e, p)).start()
        rcopy(pair_ref.at[:, cols(p)], gs.at[block(t, 16)], SLICE, (e, p)).start()

    @pl.loop(1, nt)
    def _(k):
        rcopy(pair_ref, g.at[block(t, 16)], TOKENS, (e, lax.rem(t + k, nt))).start()

    @pl.loop(1, chips)
    def _(k):
        q = lax.rem(t + 2 * k, nt)
        for h in range(2):
            for m in range(3):
                source = w_out if m == 2 else w_in.at[m]
                rcopy(source.at[:, cols(2 * (q // 2) + h)], wt.at[h, m, block(chip, hid)], WEIGHT, (e, q)).start()

    tabs[block(t, 16), :] = table_ref[...]
    gs[block(t, 16), :] = pair_ref[:, cols(t)]
    g[block(t, 16), :] = pair_ref[...]

    recv(tabs.at[pl.ds(0, (nt - 1) * 16)], TAB)
    recv(gs.at[pl.ds(0, (nt - 1) * 16)], SLICE)
    lanes = nt * 16
    chosen = tabs[...].astype(F32).T
    lane_a = lax.broadcasted_iota(jnp.int32, (lanes, lanes), 0)
    lane_b = lax.broadcasted_iota(jnp.int32, (lanes, lanes), 1)
    token_a, token_b = (lane_a // 16) * 8 + lane_a % 8, (lane_b // 16) * 8 + lane_b % 8
    earlier = jnp.where((lane_a % 16 < 8) & (token_a < token_b), 1.0, 0.0).astype(BF)
    tokens_here = gs[...]
    for chunk in range(chips):
        size = gc * m32
        row = lax.broadcasted_iota(jnp.int32, (size, lanes), 0) + chunk * size
        lane = lax.broadcasted_iota(jnp.int32, (size, lanes), 1)
        kind, slot = (row // SLOTS) % 2, (row % SLOTS).astype(F32)
        expert = (row // m32).astype(F32)
        named = jnp.zeros((size, lanes), F32)
        gate = jnp.zeros((size, lanes), F32)
        for k in range(topk):
            hit = chosen[k:k + 1, :] == expert
            named = jnp.where(hit, 1.0, named)
            gate = jnp.where(hit, chosen[topk + k:topk + k + 1, :] * (1.0 / 64.0), gate)
        rank = dot(named.astype(BF), earlier)
        here = jnp.where((rank == slot) & ((lane // 8) % 2 == kind), named, 0.0)
        there = jnp.where(kind == 1, here * gate, here).astype(BF)
        t2[pl.ds(chunk * size, size), :] = jnp.where(kind == 1, here, here * gate).astype(BF)
        snd[pl.ds(chunk * gc, gc)] = dot(there, tokens_here).astype(BF).reshape(gc, m32, d8)

    @pl.loop(1, ne)
    def _(k):
        p = lax.rem(e + k, ne)
        rcopy(snd.at[p], xr.at[core, e], DISPATCH, (p, t)).start()

    xr[core, e] = snd[e]

    recv(g.at[pl.ds(0, (nt - 1) * 16)], TOKENS)
    for copy in own_shared:
        copy.wait()
    sh = sw_out.shape[0]

    def shared_step(n, sums):
        piece = g[:, cols(n)]
        return tuple(
            total + dot(piece, weight[:, cols(n)], NT)
            for total, weight in zip(sums, (sw_in.at[0], sw_in.at[1], sw_out)))

    zero = jnp.zeros((nt * 16, sh), F32)
    sums = lax.fori_loop(0, nt, shared_step, (zero, zero, zero))
    s_gate, s_up = [v.reshape(nt, 16, sh)[:, :8].reshape(nt * 8, sh) for v in sums[:2]]
    s_back = sums[2].reshape(nt, 16, sh)[:, 8:].reshape(nt * 8, sh)
    s_act, s_slope = silu_parts(s_gate)
    s_hidden = (s_act * s_up).astype(BF)
    s_dgate = (s_back * s_up * s_slope).astype(BF)
    s_dup = (s_back * s_act).astype(BF)

    @pl.loop(0, nt)
    def _(n):
        y = dot(s_hidden, sw_out[:, cols(n)]).reshape(nt, 8, d8)
        dx = (dot(s_dgate, sw_in[0, :, cols(n)]) + dot(s_dup, sw_in[1, :, cols(n)])).reshape(nt, 8, d8)
        shs[:, :, cols(n)] = jnp.concatenate([y, dx], axis=1).astype(BF)

    partner = t + 1 - 2 * core
    recv(xr.at[core, pl.ds(0, ne - 1)], DISPATCH)
    rcopy(xr.at[core], xr.at[core], PARTNER, (e, partner)).start()
    for copy in own_weights:
        copy.wait()
    recv(wt.at[:, :, pl.ds(0, (chips - 1) * hid)], WEIGHT)

    def products(h, j):
        part = xr[h, pl.ds(j * gc, gc)]
        x_rows = part[:, :SLOTS].reshape(rows, d8)
        dy_rows = part[:, SLOTS:].reshape(rows, d8)
        return dot(x_rows, wt[h, 0], NT), dot(x_rows, wt[h, 1], NT), dot(dy_rows, wt[h, 2], NT)

    @pl.loop(0, chips)
    def _(j):
        for m, value in enumerate(products(core, j)):
            pf[j, :, m * half:(m + 1) * half] = value

    recv(xr.at[1 - core], PARTNER)

    @pl.loop(1, chips + 1)
    def _(k):
        j = lax.rem(chip + k, chips)
        for m, value in enumerate(products(1 - core, j)):
            span = slice(m * half, (m + 1) * half)
            total = pf[j, :, span] + value
            pf[j, :, span] = total
            pb[j, :, span] = total.astype(BF)

        @pl.when(k < chips)
        def _():
            rcopy(pb.at[j], rs.at[chip], PRE, (e, 2 * j + core)).start()

    recv(rs.at[pl.ds(0, chips - 1)], PRE)
    total = pf[chip]
    for k in range(1, chips):
        total = total + rs[lax.rem(chip + k, chips)].astype(F32)
    gate_pre, up_pre, back = total[:, :half], total[:, half:2 * half], total[:, 2 * half:]
    active, slope = silu_parts(gate_pre)
    act[chip, :, :half] = (active * up_pre).astype(BF)
    act[chip, :, half:2 * half] = (back * up_pre * slope).astype(BF)
    act[chip, :, 2 * half:] = (back * active).astype(BF)

    @pl.loop(1, chips)
    def _(k):
        rcopy(act.at[chip], act.at[chip], ACT, (e, lax.rem(t + 2 * k, nt))).start()

    recv(act.at[pl.ds(0, chips - 1)], ACT)

    @pl.loop(1, nt)
    def _(k):
        p = lax.rem(t + k, nt)
        rcopy(shs.at[p], shr.at[t], SHARED, (e, p)).start()

    def results(h, j):
        y = dot(act[j, :, :half], wt[h, 2])
        dx = dot(act[j, :, half:], wt[h, 0:2].reshape(2 * half, d8))
        return jnp.concatenate([y.reshape(gc, SLOTS, d8), dx.reshape(gc, SLOTS, d8)], axis=1)

    first = (e * chips) // ne

    @pl.loop(0, chips)
    def _(k):
        j = lax.rem(first + k, chips)
        ps[pl.ds(j * gc, gc)] = results(1 - core, j).astype(BF)
        rcopy(ps.at[pl.ds(j * gc, gc)], pr.at[pl.ds(j * gc, gc)], HALF + k, (e, partner)).start()

    @pl.loop(0, chips)
    def _(k):
        j = lax.rem(first + k, chips)
        value = results(core, j)
        recv(pr.at[pl.ds(j * gc, gc)], HALF + k)
        ret[pl.ds(j * gc, gc)] = (value + pr[pl.ds(j * gc, gc)].astype(F32)).astype(BF)

        @pl.loop(0, gc)
        def _(n):
            p = j * gc + n

            @pl.when(p != e)
            def _():
                rcopy(ret.at[p], bk.at[e], BACK, (p, t)).start()

    bk[e] = ret[e]

    own_grads = []
    for h in range(2):
        for m in range(3):
            right = (xr[h, :, SLOTS:] if m == 2 else xr[h, :, :SLOTS]).reshape(ne * SLOTS, d8)
            if m == 2:
                left = act[:, :, :half].reshape(chips * rows, half)
            else:
                left = act[:, :, (m + 1) * half:(m + 2) * half].reshape(chips * rows, half)
            gb[h, m] = dot(left, right, TN).astype(BF)
            target = gout_ref if m == 2 else gin_ref.at[m]
            which = GRAD_OUT if m == 2 else GRAD_IN
            own = pltpu.make_async_copy(
                gb.at[h, m, block(chip, hid)], target.at[:, cols(2 * chip + h)], lsem.at[2 + 3 * h + m])
            own.start()
            own_grads.append(own)

            @pl.loop(1, chips)
            def _(k):
                q = lax.rem(t + 2 * k, nt)
                rcopy(gb.at[h, m, block(q // 2, hid)], target.at[:, cols(2 * chip + h)], which, (e, q)).start()

    recv(bk.at[pl.ds(0, ne - 1)], BACK)
    routed = dot(t2[...], bk[...].reshape(ne * m32, d8), TN)
    fs[...] = routed.astype(BF).reshape(nt, 16, d8)

    @pl.loop(1, nt)
    def _(k):
        p = lax.rem(t + k, nt)
        rcopy(fs.at[p], fr.at[t], FINAL, (e, p)).start()

    fr[t] = fs[t]
    shr[t] = shs[t]
    recv(shr.at[pl.ds(0, nt - 1)], SHARED)
    recv(fr.at[pl.ds(0, nt - 1)], FINAL)

    for n in range(nt):
        span = slice(n * d8, (n + 1) * d8)
        total = fr[n].astype(F32) + jnp.sum(shr[:, :, span].astype(F32), axis=0)
        out_ref[:, span] = total[:8].astype(BF)
        gtok_ref[:, span] = total[8:].astype(BF)

    recv(gin_ref.at[:, :, pl.ds(0, 2 * (chips - 1) * d8)], GRAD_IN)
    recv(gout_ref.at[:, pl.ds(0, 2 * (chips - 1) * d8)], GRAD_OUT)
    for copy in own_grads:
        copy.wait()
    sent(tabs.at[pl.ds(0, (nt - 1) * 16)], TAB)
    sent(gs.at[pl.ds(0, (nt - 1) * 16)], SLICE)
    sent(g.at[pl.ds(0, (nt - 1) * 16)], TOKENS)
    sent(wt.at[:, :, pl.ds(0, (chips - 1) * hid)], WEIGHT)
    sent(snd.at[pl.ds(0, ne - 1)], DISPATCH)
    sent(xr.at[core], PARTNER)
    sent(pb.at[pl.ds(0, chips - 1)], PRE)
    sent(rs.at[pl.ds(0, chips - 1)], ACT)
    for k in range(chips):
        sent(ps.at[pl.ds(0, gc)], HALF + k)
    sent(ret.at[pl.ds(0, ne - 1)], BACK)
    sent(gin_ref.at[:, :, pl.ds(0, 2 * (chips - 1) * d8)], GRAD_IN)
    sent(gout_ref.at[:, pl.ds(0, 2 * (chips - 1) * d8)], GRAD_OUT)
    sent(shs.at[pl.ds(0, nt - 1)], SHARED)
    sent(fs.at[pl.ds(0, nt - 1)], FINAL)


def on_device(tokens, routes, gate_num, cotangent, w_in, w_out, shared_in, shared_out):
    ne, nt = lax.axis_size("expert"), lax.axis_size("tensor")
    chips = nt // 2
    own, features = tokens.shape
    topk = routes.shape[1]
    hid, sh = w_out.shape[1], shared_out.shape[0]
    d8, half, gc = features // nt, chips * hid, ne // chips
    rows, m32 = gc * SLOTS, 2 * SLOTS
    pair = jnp.concatenate([tokens, cotangent], axis=0)
    table = jnp.concatenate([routes, gate_num], axis=1)
    table = jnp.pad(jnp.concatenate([table, table], axis=0), ((0, 0), (0, 128 - 2 * topk)))
    vm = pl.BlockSpec(memory_space=pltpu.VMEM)
    hbm = pl.BlockSpec(memory_space=pl.ANY)
    scratch = [
        pltpu.VMEM((nt * 16, 128), jnp.int32),
        pltpu.VMEM((nt * 16, d8), BF),
        pltpu.VMEM((nt * 16, features), BF),
        pltpu.VMEM((2, 3, half, d8), BF),
        pltpu.VMEM((2, sh, features), BF),
        pltpu.VMEM((sh, features), BF),
        pltpu.VMEM((ne * m32, nt * 16), BF),
        pltpu.VMEM((ne, m32, d8), BF),
        pltpu.VMEM((2, ne, m32, d8), BF),
        pltpu.VMEM((chips, rows, 3 * half), F32),
        pltpu.VMEM((chips, rows, 3 * half), BF),
        pltpu.VMEM((chips, rows, 3 * half), BF),
        pltpu.VMEM((chips, rows, 3 * half), BF),
        pltpu.VMEM((ne, m32, d8), BF),
        pltpu.VMEM((ne, m32, d8), BF),
        pltpu.VMEM((ne, m32, d8), BF),
        pltpu.VMEM((ne, m32, d8), BF),
        pltpu.VMEM((2, 3, half, d8), BF),
        pltpu.VMEM((nt, 16, features), BF),
        pltpu.VMEM((nt, 16, features), BF),
        pltpu.VMEM((nt, 16, d8), BF),
        pltpu.VMEM((nt, 16, d8), BF),
        pltpu.SemaphoreType.DMA((COUNT,)),
        pltpu.SemaphoreType.DMA((COUNT,)),
        pltpu.SemaphoreType.DMA((8,)),
    ]
    out, gtok, gin, gout = pl.pallas_call(
        functools.partial(kernel, topk),
        out_shape=(
            jax.ShapeDtypeStruct((own, features), BF),
            jax.ShapeDtypeStruct((own, features), BF),
            jax.ShapeDtypeStruct((2, hid, features), BF),
            jax.ShapeDtypeStruct((hid, features), BF),
        ),
        in_specs=[vm, vm, hbm, hbm, hbm, hbm],
        out_specs=(vm, vm, hbm, hbm),
        scratch_shapes=scratch,
        compiler_params=pltpu.CompilerParams(
            collective_id=0, has_side_effects=True, vmem_limit_bytes=56 * 2**20
        ),
    )(pair, table, w_in[0], w_out[0], shared_in, shared_out)
    return out, gtok, gin[None], gout[None]


def solution(mesh):
    in_specs = (
        P(("expert", "tensor"), None),
        P(("expert", "tensor"), None),
        P(("expert", "tensor"), None),
        P(("expert", "tensor"), None),
        P("expert", None, "tensor", None),
        P("expert", "tensor", None),
        P(None, "tensor", None),
        P("tensor", None),
    )
    out_specs = (
        P(("expert", "tensor"), None),
        P(("expert", "tensor"), None),
        P("expert", None, "tensor", None),
        P("expert", "tensor", None),
    )
    return jax.shard_map(
        on_device, mesh=mesh, in_specs=in_specs, out_specs=out_specs, check_vma=False
    )
```

time: 616 us -> 158 us (0.26)
  waiting for transfers between devices: 435 us -> 0 us
  Pallas kernels: 0 us -> 147 us
  matrix products: 63.4 us -> 0 us
  blocking collectives: 56.1 us -> 0 us
  starting transfers between devices: 42 us -> 0 us
  between operations: 14.3 us -> 0.64 us
  local copies, waits for them, and re-layouts: 0.84 us -> 7.64 us
    all_to_all x4 -> x0, waiting for transfers between devices: 410 us -> none  [the longest x1 108 us: on_device(): lax.all_to_all(out_part, 'expert', split_axis=0, concat_axis=0, tiled=True)]
    pallas_call x0 -> x1, Pallas kernels: none -> 147 us  [on_device(): pl.pallas_call(functools.partial(kernel, topk), out_shape=(jax.ShapeDtype...]
    dot_general x19 -> x0, matrix products: 63.4 us -> none  [the longest x6 21.5 us: contract_last(): lax.dot_general(left, right, (((1,), (1,)), ((), ())), preferred_element_...]
    all_gather x4 -> x0, blocking collectives: 56.1 us -> none  [the longest x1 16.1 us: on_device(): lax.all_gather(routes, 'tensor', axis=0, tiled=True)]
    all_to_all x4 -> x0, starting transfers between devices: 42 us -> none  [the longest x1 12.4 us: on_device(): lax.all_to_all(out_part, 'expert', split_axis=0, concat_axis=0, tiled=True)]
    reduce_scatter x2 -> x0, waiting for transfers between devices: 25 us -> none  [the longest x1 25 us: on_device(): lax.psum_scatter((shared_dx + routed_dx).astype(jnp.bfloat16), 'tensor',...]
    unnamed x26 -> x6, local copies, waits for them, and re-layouts: 0.07 us -> 7.03 us
  transfers between devices with their start and end apart: 6 -> 0, of which waited for: 5 -> 0; matrix products, arithmetic and copies ran while one was open for 8% -> 0% of each run, Pallas kernels for 0% -> 0%
where the time goes in v1:
time: 158 us; the launch traced here: 157 us
  Pallas kernels  147 us (93%)
  local copies, waits for them, and re-layouts  7.64 us (5%)
  other arithmetic  2.44 us (2%)
    pallas_call x1, Pallas kernels, on_device(): pl.pallas_call(functools.partial(kernel, topk), out_shape=(jax.ShapeDtype...  147 us
    unnamed x6, local copies, waits for them, and re-layouts  7.03 us

profile of v1, /device:TPU:1, one launch (start us, length us, event | category | flops | bytes accessed | tf_op | source)
XLA Modules:
  0.0 157.4 jit_solution(13996555559632299393)
XLA Ops:
  0.6 0.8 add_add_fusion
  1.5 0.6 pad.4.table_ref
  2.1 1.6 %pad_maximum_fusion.pair_ref = bf16[16,5120]{1,0:T(8,128)(2,1)} fusion(bf16[8,5120]{1,0:T(8,128)(2,1)} %param.11, bf16[8,5120]{1,0:T(8,128)(2,1)} %param.8), kind=kLoop, calls=%fused_computation | loop fusion | flops 327680 | bytes 327680 | tf_op jit(solution)/shard_map/concatenate | solution.py:329
  3.7 146.7 %shard_map.111 = (bf16[8,5120]{1,0:T(8,128)(2,1)}, bf16[8,5120]{1,0:T(8,128)(2,1)}, bf16[2,96,5120]{2,1,0:T(8,128)(2,1)}, bf16[96,5120]{1,0:T(8,128)(2,1)}) custom-call(bf16[16,5120]{1,0:T(8,128)(2,1)} %pad_maximum_fusion.pair_ref, s32[16,128]{1,0:T(8,128)} %pad.4.table_ref, bf16[2,96,5120]{2,1,0:T(8,128)(2,1)} %bitcast.4, bf16[96,5120]{1,0:T(8,128)(2,1)} %bitcast.6, ...), custom_call_target="tpu_custom_call" | custom-call | tf_op jit(solution)/shard_map/pallas_call | solution.py:361
  150.4 1.5 copy.16
  151.9 1.5 copy.17
  153.5 0.0 copy-start
  153.5 3.0 %copy.18 = bf16[1,2,96,5120]{3,2,1,0:T(8,128)(2,1)} copy(bf16[1,2,96,5120]{3,2,1,0:T(8,128)(2,1)} %bitcast.5) | data formatting | bytes 3932160
  156.5 0.0 copy-done
  156.5 0.9 copy.19
Async XLA Ops:
  153.5 3.0 %copy-start = (bf16[96,5120]{1,0:T(8,128)(2,1)S(1)}, bf16[96,5120]{1,0:T(8,128)(2,1)}, u32[]{:S(2)}) copy-start(bf16[96,5120]{1,0:T(8,128)(2,1)} %get-tuple-element.11) | copy-start | bytes 2949124

commit v2 on v1

v2 whole, which is shorter than its diff:
```python
import functools

import jax
import jax.numpy as jnp
from jax import lax
from jax.experimental import pallas as pl
from jax.experimental.pallas import tpu as pltpu
from jax.sharding import PartitionSpec as P

MESH = pl.DeviceIdType.MESH
BF = jnp.bfloat16
F32 = jnp.float32
SLOTS = 16
NT = (((1,), (1,)), ((), ()))
TN = (((0,), (0,)), ((), ()))

TAB, SLICE, TOKX, TOKP, WPART, XP, PRE, ACT, ACTP, BACK, GRAD_IN, GRAD_OUT, SHP, SHARED, FINAL = range(15)
WX, WF, DISP, PAIR, HALF = 15, 17, 19, 23, 27
COUNT = 31


def dot(left, right, dims=None):
    dims = dims or (((1,), (0,)), ((), ()))
    return lax.dot_general(left, right, dims, preferred_element_type=F32)


def silu_parts(preact):
    sig_value = jax.nn.sigmoid(preact)
    return preact * sig_value, sig_value * (1.0 + preact * (1.0 - sig_value))


def kernel(
    topk,
    tok_ref, cot_ref, routes_ref, gates_ref, w_in, w_out, sh_in, sh_out,
    out_ref, gtok_ref, gin_ref, gout_ref,
    pair, table, tabs, gs, g, wt, sw_in, sw_out, t2, snd, xr, xp, pf, pb, rs, act, actp, ps, pr, po, ret, bk, gb,
    shs, shp, shr, fs, fr, ssem, rsem, lsem,
):
    ne, nt = lax.axis_size("expert"), lax.axis_size("tensor")
    e, t = lax.axis_index("expert"), lax.axis_index("tensor")
    chip, core = t // 2, t % 2
    chips = nt // 2
    a, q = chip // 2, chip % 2
    partner = t + 1 - 2 * core
    row_chip = 2 * a + 1 - q
    weight_chip = chips - 1 - chip
    row_dev, weight_dev = (e, 2 * row_chip + core), (e, 2 * weight_chip + core)
    first = (e * chips) // ne
    stays = e % 2 == core
    d8 = gs.shape[1]
    hid = w_out.shape[0]
    half = 4 * hid
    gl_count = ne // 2
    gq = gl_count // 4
    rows = 2 * gq * SLOTS
    m32 = 2 * SLOTS

    def rcopy(src, dst, which, dev):
        return pltpu.make_async_remote_copy(
            src_ref=src, dst_ref=dst, send_sem=ssem.at[which], recv_sem=rsem.at[which],
            device_id=dev, device_id_type=MESH,
        )

    def recv(ref, which):
        pltpu.make_async_copy(ref, ref, rsem.at[which]).wait()

    def sent(ref, which):
        pltpu.make_async_copy(ref, ref, ssem.at[which]).wait()

    def cols(piece):
        return pl.ds(pl.multiple_of(piece * d8, 128), d8)

    def block(index, size):
        return pl.ds(pl.multiple_of(index * size, 16), size)

    def source(m):
        return w_out if m == 2 else w_in.at[m]

    place = 2 * a + core
    own_shared = [
        pltpu.make_async_copy(sh_in, sw_in, lsem.at[0]),
        pltpu.make_async_copy(sh_out, sw_out, lsem.at[1]),
    ]
    own_weights = [
        pltpu.make_async_copy(
            source(m).at[:, cols(4 * a + 2 * n + h)], wt.at[n, h, m, block(place, hid)], lsem.at[2 + 6 * n + 3 * h + m])
        for n in range(2) for h in range(2) for m in range(3)]

    barrier = pltpu.get_barrier_semaphore()

    @pl.loop(1, nt)
    def _(k):
        pl.semaphore_signal(barrier, inc=1, device_id=(e, lax.rem(t + k, nt)), device_id_type=MESH)

    @pl.loop(1, ne)
    def _(k):
        for h in range(2):
            pl.semaphore_signal(barrier, inc=1, device_id=(lax.rem(e + k, ne), 2 * chip + h), device_id_type=MESH)

    for copy in own_weights + own_shared:
        copy.start()
    for n in range(nt):
        span = slice(n * d8, (n + 1) * d8)
        pair[:, span] = jnp.concatenate(
            [tok_ref[:, span].astype(F32), cot_ref[:, span].astype(F32)], axis=0).astype(BF)
    table[...] = jnp.zeros_like(table)
    for n in range(2):
        table[8 * n:8 * n + 8, :topk] = routes_ref[...]
        table[8 * n:8 * n + 8, topk:2 * topk] = gates_ref[...]

    pl.semaphore_wait(barrier, 2 * (ne - 1) + nt - 1)

    @pl.loop(1, nt)
    def _(k):
        p = lax.rem(t + k, nt)
        rcopy(table, tabs.at[block(t, 16)], TAB, (e, p)).start()
        rcopy(pair.at[:, cols(p)], gs.at[block(t, 16)], SLICE, (e, p)).start()

    @pl.loop(1, chips)
    def _(k):
        rcopy(pair, g.at[block(t, 16)], TOKX, (e, lax.rem(t + 2 * k, nt))).start()

    rcopy(pair, g.at[block(t, 16)], TOKP, (e, partner)).start()
    for n in range(2):
        there = n * q + (1 - n) * (1 - q)
        for h in range(2):
            for m in range(3):
                rcopy(source(m).at[:, cols(4 * (1 - a) + 2 * there + h)], wt.at[there, h, m, block(place, hid)],
                      WX + n, weight_dev).start()
    for n in range(2):
        for h in range(2):
            for m in range(3):
                rcopy(source(m).at[:, cols(4 * a + 2 * n + h)], wt.at[n, h, m, block(place, hid)],
                      WPART, (e, partner)).start()

    tabs[block(t, 16), :] = table[...]
    gs[block(t, 16), :] = pair[:, cols(t)]
    g[block(t, 16), :] = pair[...]

    recv(tabs.at[pl.ds(0, (nt - 1) * 16)], TAB)
    lanes = nt * 16
    chosen = tabs[...].astype(F32).T
    lane_a = lax.broadcasted_iota(jnp.int32, (lanes, lanes), 0)
    lane_b = lax.broadcasted_iota(jnp.int32, (lanes, lanes), 1)
    token_a, token_b = (lane_a // 16) * 8 + lane_a % 8, (lane_b // 16) * 8 + lane_b % 8
    earlier = jnp.where((lane_a % 16 < 8) & (token_a < token_b), 1.0, 0.0).astype(BF)
    recv(gs.at[pl.ds(0, (nt - 1) * 16)], SLICE)
    tokens_here = gs[...]
    ec = ne // 4
    size = ec * m32
    for turn in range(4):
        chunk = lax.rem(first + turn, 4)
        row = lax.broadcasted_iota(jnp.int32, (size, lanes), 0)
        lane = lax.broadcasted_iota(jnp.int32, (size, lanes), 1)
        kind, slot = (row // SLOTS) % 2, (row % SLOTS).astype(F32)
        expert = (row // m32 + chunk * ec).astype(F32)
        named = jnp.zeros((size, lanes), F32)
        gate = jnp.zeros((size, lanes), F32)
        for k in range(topk):
            hit = chosen[k:k + 1, :] == expert
            named = jnp.where(hit, 1.0, named)
            gate = jnp.where(hit, chosen[topk + k:topk + k + 1, :] * (1.0 / 64.0), gate)
        rank = dot(named.astype(BF), earlier)
        here = jnp.where((rank == slot) & ((lane // 8) % 2 == kind), named, 0.0)
        weighted = jnp.where(kind == 1, here * gate, here).astype(BF)
        t2[block(chunk, size), :] = jnp.where(kind == 1, here, here * gate).astype(BF)
        snd[pl.ds(chunk * ec, ec)] = dot(weighted, tokens_here).astype(BF).reshape(ec, m32, d8)

        @pl.loop(0, ec)
        def _(n):
            p = chunk * ec + n
            target = xr.at[q, core, e // 2]

            @pl.when(jnp.logical_and(p == e, stays))
            def _():
                pltpu.make_async_copy(snd.at[p], target, rsem.at[DISP + first]).start()

            @pl.when(jnp.logical_not(jnp.logical_and(p == e, stays)))
            def _():
                rcopy(snd.at[p], target, DISP + first, (p, 2 * chip + e % 2)).start()

    def pass_rows(k):
        chunk = lax.rem(first + 4 - k, 4)
        part = xr.at[q, :, pl.ds(chunk * gq, gq)]
        recv(part, DISP + chunk)
        rcopy(part, part, PAIR + k, row_dev).start()

    def pass_weights(n):
        there = n * (1 - q) + (1 - n) * q
        part = wt.at[there, :, :, block(2 * (1 - a) + core, hid)]
        recv(part, WX + n)
        rcopy(part, part, WF + n, (e, partner)).start()

    recv(g.at[pl.ds(0, (chips - 1) * 16)], TOKX)

    @pl.loop(1, chips)
    def _(k):
        part = g.at[block(lax.rem(t + 2 * k, nt), 16)]
        rcopy(part, part, TOKP, (e, partner)).start()

    pass_rows(0)
    recv(g.at[pl.ds(0, chips * 16)], TOKP)
    for copy in own_shared:
        copy.wait()
    sh = sw_out.shape[0]

    def shared_step(n, sums):
        piece = g[:, cols(n)]
        return tuple(
            total + dot(piece, weight[:, cols(n)], NT)
            for total, weight in zip(sums, (sw_in.at[0], sw_in.at[1], sw_out)))

    zero = jnp.zeros((nt * 16, sh), F32)
    sums = lax.fori_loop(0, nt, shared_step, (zero, zero, zero))
    pass_rows(1)
    s_gate, s_up = [v.reshape(nt, 16, sh)[:, :8].reshape(nt * 8, sh) for v in sums[:2]]
    s_back = sums[2].reshape(nt, 16, sh)[:, 8:].reshape(nt * 8, sh)
    s_act, s_slope = silu_parts(s_gate)
    s_hidden = (s_act * s_up).astype(BF)
    s_dgate = (s_back * s_up * s_slope).astype(BF)
    s_dup = (s_back * s_act).astype(BF)

    def shared_terms(low, high):
        @pl.loop(low, high)
        def _(n):
            y = dot(s_hidden, sw_out[:, cols(n)]).reshape(nt, 8, d8)
            dx = (dot(s_dgate, sw_in[0, :, cols(n)]) + dot(s_dup, sw_in[1, :, cols(n)])).reshape(nt, 8, d8)
            shs[:, :, :, cols(n)] = jnp.concatenate([y, dx], axis=1).astype(BF).reshape(chips, 2, 16, d8)

    shared_terms(0, nt // 2)
    pass_weights(0)
    pass_rows(2)
    shared_terms(nt // 2, nt)
    rcopy(shs.at[:, 1 - core], shp, SHP, (e, partner)).start()
    pass_rows(3)
    pass_weights(1)

    def products(quarter, n):
        value = [None] * 3
        for h in range(2):
            part = xr[quarter, h, pl.ds(n * 2 * gq, 2 * gq)]
            x_rows = part[:, :SLOTS].reshape(rows, d8)
            dy_rows = part[:, SLOTS:].reshape(rows, d8)
            for m in range(3):
                term = dot(dy_rows if m == 2 else x_rows, wt[quarter, h, m], NT)
                value[m] = term if h == 0 else value[m] + term
        return value

    for copy in own_weights:
        copy.wait()
    recv(wt.at[:, :, :, pl.ds(0, hid)], WPART)
    recv(wt.at[0, :, :, pl.ds(0, hid)], WF)

    @pl.loop(0, 2)
    def _(n):
        for m, value in enumerate(products(q, n)):
            pf[n, :, m * half:(m + 1) * half] = value

    recv(shp, SHP)
    for n in range(chips):
        shs[n, core] = (shs[n, core].astype(F32) + shp[n].astype(F32)).astype(BF)

    recv(wt.at[0, :, :, pl.ds(0, hid)], WF + 1)
    for k in range(4):
        recv(xr.at[0, :, pl.ds(0, gq)], PAIR + k)

    def finish(n):
        for m, value in enumerate(products(1 - q, n)):
            span = slice(m * half, (m + 1) * half)
            pf[n, :, span] = pf[n, :, span] + value

    finish(1 - a)
    pb[...] = pf[1 - a].astype(BF)
    rcopy(pb, rs, PRE, weight_dev).start()
    rcopy(xr.at[:, 1 - core], xp, XP, (e, partner)).start()

    @pl.loop(1, chips)
    def _(k):
        j = lax.rem(chip + k, chips)
        rcopy(shs.at[j, core], shr.at[chip], SHARED, (e, 2 * j + core)).start()

    finish(a)
    recv(rs, PRE)
    total = pf[a] + rs[...].astype(F32)
    gate_pre, up_pre, back = total[:, :half], total[:, half:2 * half], total[:, 2 * half:]
    active, slope = silu_parts(gate_pre)
    act[a, :, :half] = (active * up_pre).astype(BF)
    act[a, :, half:2 * half] = (back * up_pre * slope).astype(BF)
    act[a, :, 2 * half:] = (back * active).astype(BF)
    rcopy(act.at[a], act.at[a], ACT, weight_dev).start()
    recv(act.at[1 - a], ACT)
    rcopy(act, actp, ACTP, (e, partner)).start()

    def results(quarter, h, n):
        y = dot(act[n, :, :half], wt[quarter, h, 2])
        dx = dot(act[n, :, half:], wt[quarter, h, 0:2].reshape(2 * half, d8))
        return jnp.concatenate([y.reshape(2 * gq, SLOTS, d8), dx.reshape(2 * gq, SLOTS, d8)], axis=1)

    def order(k):
        n = lax.rem(first // 2 + k // 2, 2)
        return 2 * n + lax.rem(first + k, 2)

    for k in range(2):
        n = lax.rem(first // 2 + k, 2)
        for h in range(2):
            ps[h, pl.ds(n * 2 * gq, 2 * gq)] = results(1 - q, h, n).astype(BF)
        for i in range(2):
            part = pl.ds(order(2 * k + i) * gq, gq)
            rcopy(ps.at[:, part], pr.at[:, part], HALF + 2 * k + i, row_dev).start()

    @pl.loop(0, 2)
    def _(n):
        for h in range(2):
            po[h, pl.ds(n * 2 * gq, 2 * gq)] = results(q, h, n)

    recv(xp, XP)
    recv(actp, ACTP)
    own_grads = []

    def gradient(n, m):
        span = slice(0, half) if m == 2 else slice((m + 1) * half, (m + 2) * half)
        kind = slice(SLOTS, m32) if m == 2 else slice(0, SLOTS)
        here = act[:, :, span].reshape(2 * rows, half)
        there = actp[:, :, span].reshape(2 * rows, half)
        x_here = xr[n, core, :, kind].reshape(2 * rows, d8)
        x_there = xp[n, :, kind].reshape(2 * rows, d8)
        gb[n, m] = (dot(here, x_here, TN) + dot(there, x_there, TN)).astype(BF)
        target = (gout_ref if m == 2 else gin_ref.at[m]).at[:, cols(4 * a + 2 * n + core)]
        which = GRAD_OUT if m == 2 else GRAD_IN
        for c in range(2):
            rcopy(gb.at[n, m, block(2 * (1 - a) + c, hid)], target, which, (e, 2 * weight_chip + c)).start()
        rcopy(gb.at[n, m, block(2 * a + 1 - core, hid)], target, which, (e, partner)).start()
        own = pltpu.make_async_copy(gb.at[n, m, block(place, hid)], target, lsem.at[2 + 3 * n + m])
        own.start()
        own_grads.append(own)

    def give_back(k):
        chunk = order(k)
        part = pl.ds(chunk * gq, gq)
        recv(pr.at[:, part], HALF + k)
        ret[:, part] = (po[:, part] + pr[:, part].astype(F32)).astype(BF)

        @pl.loop(0, gq)
        def _(n):
            place_here = chunk * gq + n
            p = 2 * place_here + core
            for h in range(2):
                local = jnp.logical_and(p == e, core == h)

                @pl.when(local)
                def _():
                    pltpu.make_async_copy(ret.at[h, place_here], bk.at[e], rsem.at[BACK]).start()

                @pl.when(jnp.logical_not(local))
                def _():
                    rcopy(ret.at[h, place_here], bk.at[e], BACK, (p, 2 * chip + h)).start()

    for m in range(3):
        gradient(0, m)
    give_back(0)
    gradient(1, 0)
    gradient(1, 1)
    give_back(1)
    gradient(1, 2)
    give_back(2)
    give_back(3)

    recv(bk, BACK)
    routed = dot(t2[...], bk[...].reshape(ne * m32, d8), TN)
    fs[...] = routed.astype(BF).reshape(nt, 16, d8)

    @pl.loop(1, nt)
    def _(k):
        p = lax.rem(t + k, nt)
        rcopy(fs.at[p], fr.at[t], FINAL, (e, p)).start()

    fr[t] = fs[t]
    shr[chip] = shs[chip, core]
    recv(shr.at[pl.ds(0, chips - 1)], SHARED)
    recv(fr.at[pl.ds(0, nt - 1)], FINAL)

    for n in range(nt):
        span = slice(n * d8, (n + 1) * d8)
        total = fr[n].astype(F32) + jnp.sum(shr[:, :, span].astype(F32), axis=0)
        out_ref[:, span] = total[:8].astype(BF)
        gtok_ref[:, span] = total[8:].astype(BF)

    recv(gin_ref.at[:, :, pl.ds(0, 6 * d8)], GRAD_IN)
    recv(gout_ref.at[:, pl.ds(0, 6 * d8)], GRAD_OUT)
    for copy in own_grads:
        copy.wait()
    sent(tabs.at[pl.ds(0, (nt - 1) * 16)], TAB)
    sent(gs.at[pl.ds(0, (nt - 1) * 16)], SLICE)
    sent(g.at[pl.ds(0, (chips - 1) * 16)], TOKX)
    sent(g.at[pl.ds(0, chips * 16)], TOKP)
    sent(wt.at[:, :, :, pl.ds(0, hid)], WPART)
    for n in range(2):
        sent(wt.at[n, :, :, pl.ds(0, hid)], WX + n)
        sent(wt.at[n, :, :, pl.ds(0, hid)], WF + n)
    for k in range(4):
        sent(xr.at[0, :, pl.ds(0, gq)], PAIR + k)
        sent(ps.at[:, pl.ds(0, gq)], HALF + k)
    sent(xp, XP)
    sent(rs, PRE)
    sent(act.at[0], ACT)
    sent(actp, ACTP)
    sent(shp, SHP)
    sent(shr.at[pl.ds(0, chips - 1)], SHARED)
    sent(gin_ref.at[:, :, pl.ds(0, 6 * d8)], GRAD_IN)
    sent(gout_ref.at[:, pl.ds(0, 6 * d8)], GRAD_OUT)
    sent(fs.at[pl.ds(0, nt - 1)], FINAL)

    @pl.when(stays)
    def _():
        sent(bk.at[pl.ds(0, ne - 1)], BACK)
        sent(bk.at[pl.ds(0, ne - 1)], DISP + first)

    @pl.when(jnp.logical_not(stays))
    def _():
        sent(bk, BACK)
        sent(bk, DISP + first)


def on_device(tokens, routes, gate_num, cotangent, w_in, w_out, shared_in, shared_out):
    ne, nt = lax.axis_size("expert"), lax.axis_size("tensor")
    chips = nt // 2
    own, features = tokens.shape
    topk = routes.shape[1]
    hid, sh = w_out.shape[1], shared_out.shape[0]
    d8, half, gl_count = features // nt, 4 * hid, ne // 2
    rows, m32 = gl_count * SLOTS // 2, 2 * SLOTS
    vm = pl.BlockSpec(memory_space=pltpu.VMEM)
    hbm = pl.BlockSpec(memory_space=pl.ANY)
    scratch = [
        pltpu.VMEM((16, features), BF),
        pltpu.VMEM((16, 128), jnp.int32),
        pltpu.VMEM((nt * 16, 128), jnp.int32),
        pltpu.VMEM((nt * 16, d8), BF),
        pltpu.VMEM((nt * 16, features), BF),
        pltpu.VMEM((2, 2, 3, half, d8), BF),
        pltpu.VMEM((2, sh, features), BF),
        pltpu.VMEM((sh, features), BF),
        pltpu.VMEM((ne * m32, nt * 16), BF),
        pltpu.VMEM((ne, m32, d8), BF),
        pltpu.VMEM((2, 2, gl_count, m32, d8), BF),
        pltpu.VMEM((2, gl_count, m32, d8), BF),
        pltpu.VMEM((2, rows, 3 * half), F32),
        pltpu.VMEM((rows, 3 * half), BF),
        pltpu.VMEM((rows, 3 * half), BF),
        pltpu.VMEM((2, rows, 3 * half), BF),
        pltpu.VMEM((2, rows, 3 * half), BF),
        pltpu.VMEM((2, gl_count, m32, d8), BF),
        pltpu.VMEM((2, gl_count, m32, d8), BF),
        pltpu.VMEM((2, gl_count, m32, d8), F32),
        pltpu.VMEM((2, gl_count, m32, d8), BF),
        pltpu.VMEM((ne, m32, d8), BF),
        pltpu.VMEM((2, 3, half, d8), BF),
        pltpu.VMEM((chips, 2, 16, features), BF),
        pltpu.VMEM((chips, 16, features), BF),
        pltpu.VMEM((chips, 16, features), BF),
        pltpu.VMEM((nt, 16, d8), BF),
        pltpu.VMEM((nt, 16, d8), BF),
        pltpu.SemaphoreType.DMA((COUNT,)),
        pltpu.SemaphoreType.DMA((COUNT,)),
        pltpu.SemaphoreType.DMA((14,)),
    ]
    shapes = (
        jax.ShapeDtypeStruct((own, features), BF),
        jax.ShapeDtypeStruct((own, features), BF),
        jax.ShapeDtypeStruct((2, hid, features), BF),
        jax.ShapeDtypeStruct((hid, features), BF),
    )
    results = pl.pallas_call(
        functools.partial(kernel, topk),
        out_shape=shapes,
        in_specs=[vm, vm, vm, vm, hbm, hbm, hbm, hbm],
        out_specs=(vm, vm, hbm, hbm),
        scratch_shapes=scratch,
        compiler_params=pltpu.CompilerParams(
            collective_id=0, has_side_effects=True, vmem_limit_bytes=56 * 2**20
        ),
    )(tokens, cotangent, routes, gate_num, w_in[0], w_out[0], shared_in, shared_out)
    out, gtok, gin, gout = results
    return out, gtok, gin[None], gout[None]


def solution(mesh):
    in_specs = (
        P(("expert", "tensor"), None),
        P(("expert", "tensor"), None),
        P(("expert", "tensor"), None),
        P(("expert", "tensor"), None),
        P("expert", None, "tensor", None),
        P("expert", "tensor", None),
        P(None, "tensor", None),
        P("tensor", None),
    )
    out_specs = (
        P(("expert", "tensor"), None),
        P(("expert", "tensor"), None),
        P("expert", None, "tensor", None),
        P("expert", "tensor", None),
    )
    return jax.shard_map(
        on_device, mesh=mesh, in_specs=in_specs, out_specs=out_specs, check_vma=False
    )
```

time: 158 us -> 152 us (0.962)
  the two profiles are of different devices: /device:TPU:1 before, /device:TPU:33 now
where the time goes in v2:
time: 152 us
  Pallas kernels  144 us (95%)
  local copies, waits for them, and re-layouts  7.03 us (5%)
    pallas_call x1, Pallas kernels, on_device(): pl.pallas_call(functools.partial(kernel, topk), out_shape=shapes, in_spec...  144 us
    unnamed x6, local copies, waits for them, and re-layouts  7.03 us

profile of v2, /device:TPU:33, one launch (start us, length us, event | category | flops | bytes accessed | tf_op | source)
XLA Modules:
  0.0 151.9 jit_solution(7114147440745497161)
XLA Ops:
  0.6 144.2 %shard_map.111 = (bf16[8,5120]{1,0:T(8,128)(2,1)}, bf16[8,5120]{1,0:T(8,128)(2,1)}, bf16[2,96,5120]{2,1,0:T(8,128)(2,1)}, bf16[96,5120]{1,0:T(8,128)(2,1)}) custom-call(bf16[8,5120]{1,0:T(8,128)(2,1)} %tok_ref.1, bf16[8,5120]{1,0:T(8,128)(2,1)} %cot_ref.1, s32[8,6]{1,0:T(8,128)} %routes_ref.1, s32[8,6]{1,0:T(8,128)} %gates_ref.1, ...), custom_call_target="tpu_custom_call" | custom-call | tf_op jit(solution)/shard_map/pallas_call | solution.py:473
  144.8 1.5 %copy.16 = bf16[8,5120]{1,0:T(8,128)(2,1)} copy(bf16[8,5120]{1,0:T(8,128)(2,1)} %get-tuple-element.16) | data formatting | bytes 163840
  146.4 1.5 %copy.17 = bf16[8,5120]{1,0:T(8,128)(2,1)} copy(bf16[8,5120]{1,0:T(8,128)(2,1)} %get-tuple-element.17) | data formatting | bytes 163840
  147.9 0.0 copy-start
  147.9 3.0 %copy.18 = bf16[1,2,96,5120]{3,2,1,0:T(8,128)(2,1)} copy(bf16[1,2,96,5120]{3,2,1,0:T(8,128)(2,1)} %bitcast.5) | data formatting | bytes 3932160
  150.9 0.0 copy-done
  150.9 0.9 copy.19
Async XLA Ops:
  147.9 3.0 %copy-start = (bf16[96,5120]{1,0:T(8,128)(2,1)S(1)}, bf16[96,5120]{1,0:T(8,128)(2,1)}, u32[]{:S(2)}) copy-start(bf16[96,5120]{1,0:T(8,128)(2,1)} %get-tuple-element.11) | copy-start | bytes 2949124

commit v3 on v2

--- a/solution.py
+++ b/solution.py
@@ -14,9 +14,9 @@
 NT = (((1,), (1,)), ((), ()))
 TN = (((0,), (0,)), ((), ()))
 
-TAB, SLICE, TOKX, TOKP, WPART, XP, PRE, ACT, ACTP, BACK, GRAD_IN, GRAD_OUT, SHP, SHARED, FINAL = range(15)
-WX, WF, DISP, PAIR, HALF = 15, 17, 19, 23, 27
-COUNT = 31
+TAB, SLICE, TOKX, TOKP, WPART, XP, ACTP, BACK, GRAD_IN, GRAD_OUT, SHP, SHARED, FINAL = range(13)
+PRE, ACT, WX, WF, DISP, PAIR, HALF = 13, 15, 17, 19, 21, 25, 29
+COUNT = 33
 
 
 def dot(left, right, dims=None):
@@ -45,8 +45,10 @@
     row_chip = 2 * a + 1 - q
     weight_chip = chips - 1 - chip
     row_dev, weight_dev = (e, 2 * row_chip + core), (e, 2 * weight_chip + core)
-    first = (e * chips) // ne
-    stays = e % 2 == core
+    first = e % 4
+    stays = (e // 4) % 2 == core
+    home = (e % 4) * (ne // 4) + e // 4
+    local_group = (e % 4) * (ne // 8) + e // 8
     d8 = gs.shape[1]
     hid = w_out.shape[0]
     half = 4 * hid
@@ -153,7 +155,7 @@
         row = lax.broadcasted_iota(jnp.int32, (size, lanes), 0)
         lane = lax.broadcasted_iota(jnp.int32, (size, lanes), 1)
         kind, slot = (row // SLOTS) % 2, (row % SLOTS).astype(F32)
-        expert = (row // m32 + chunk * ec).astype(F32)
+        expert = (row // m32 * 4 + chunk).astype(F32)
         named = jnp.zeros((size, lanes), F32)
         gate = jnp.zeros((size, lanes), F32)
         for k in range(topk):
@@ -168,16 +170,17 @@
 
         @pl.loop(0, ec)
         def _(n):
-            p = chunk * ec + n
-            target = xr.at[q, core, e // 2]
+            p = n * 4 + chunk
+            from_here = snd.at[chunk * ec + n]
+            target = xr.at[q, core, local_group]
 
             @pl.when(jnp.logical_and(p == e, stays))
             def _():
-                pltpu.make_async_copy(snd.at[p], target, rsem.at[DISP + first]).start()
+                pltpu.make_async_copy(from_here, target, rsem.at[DISP + first]).start()
 
             @pl.when(jnp.logical_not(jnp.logical_and(p == e, stays)))
             def _():
-                rcopy(snd.at[p], target, DISP + first, (p, 2 * chip + e % 2)).start()
+                rcopy(from_here, target, DISP + first, (p, 2 * chip + (e // 4) % 2)).start()
 
     def pass_rows(k):
         chunk = lax.rem(first + 4 - k, 4)
@@ -260,6 +263,8 @@
     for n in range(chips):
         shs[n, core] = (shs[n, core].astype(F32) + shp[n].astype(F32)).astype(BF)
 
+    for j in (weight_chip, lax.rem(chip + 2, chips)):
+        rcopy(shs.at[j, core], shr.at[chip], SHARED, (e, 2 * j + core)).start()
     recv(wt.at[0, :, :, pl.ds(0, hid)], WF + 1)
     for k in range(4):
         recv(xr.at[0, :, pl.ds(0, gq)], PAIR + k)
@@ -271,24 +276,25 @@
 
     finish(1 - a)
     pb[...] = pf[1 - a].astype(BF)
-    rcopy(pb, rs, PRE, weight_dev).start()
+    for i in range(2):
+        part = pl.ds(i * (rows // 2), rows // 2)
+        rcopy(pb.at[part], rs.at[part], PRE + i, weight_dev).start()
     rcopy(xr.at[:, 1 - core], xp, XP, (e, partner)).start()
 
-    @pl.loop(1, chips)
-    def _(k):
-        j = lax.rem(chip + k, chips)
-        rcopy(shs.at[j, core], shr.at[chip], SHARED, (e, 2 * j + core)).start()
-
+    rcopy(shs.at[row_chip, core], shr.at[chip], SHARED, row_dev).start()
     finish(a)
-    recv(rs, PRE)
-    total = pf[a] + rs[...].astype(F32)
-    gate_pre, up_pre, back = total[:, :half], total[:, half:2 * half], total[:, 2 * half:]
-    active, slope = silu_parts(gate_pre)
-    act[a, :, :half] = (active * up_pre).astype(BF)
-    act[a, :, half:2 * half] = (back * up_pre * slope).astype(BF)
-    act[a, :, 2 * half:] = (back * active).astype(BF)
-    rcopy(act.at[a], act.at[a], ACT, weight_dev).start()
-    recv(act.at[1 - a], ACT)
+    for i in range(2):
+        part = pl.ds(i * (rows // 2), rows // 2)
+        recv(rs.at[part], PRE + i)
+        total = pf[a, part] + rs[part].astype(F32)
+        gate_pre, up_pre, back = total[:, :half], total[:, half:2 * half], total[:, 2 * half:]
+        active, slope = silu_parts(gate_pre)
+        act[a, part, :half] = (active * up_pre).astype(BF)
+        act[a, part, half:2 * half] = (back * up_pre * slope).astype(BF)
+        act[a, part, 2 * half:] = (back * active).astype(BF)
+        rcopy(act.at[a, part], act.at[a, part], ACT + i, weight_dev).start()
+    for i in range(2):
+        recv(act.at[1 - a, pl.ds(i * (rows // 2), rows // 2)], ACT + i)
     rcopy(act, actp, ACTP, (e, partner)).start()
 
     def results(quarter, h, n):
@@ -343,17 +349,17 @@
         @pl.loop(0, gq)
         def _(n):
             place_here = chunk * gq + n
-            p = 2 * place_here + core
+            p = 4 * (2 * n + core) + chunk
             for h in range(2):
                 local = jnp.logical_and(p == e, core == h)
 
                 @pl.when(local)
                 def _():
-                    pltpu.make_async_copy(ret.at[h, place_here], bk.at[e], rsem.at[BACK]).start()
+                    pltpu.make_async_copy(ret.at[h, place_here], bk.at[home], rsem.at[BACK]).start()
 
                 @pl.when(jnp.logical_not(local))
                 def _():
-                    rcopy(ret.at[h, place_here], bk.at[e], BACK, (p, 2 * chip + h)).start()
+                    rcopy(ret.at[h, place_here], bk.at[home], BACK, (p, 2 * chip + h)).start()
 
     for m in range(3):
         gradient(0, m)
@@ -401,8 +407,9 @@
         sent(xr.at[0, :, pl.ds(0, gq)], PAIR + k)
         sent(ps.at[:, pl.ds(0, gq)], HALF + k)
     sent(xp, XP)
-    sent(rs, PRE)
-    sent(act.at[0], ACT)
+    for i in range(2):
+        sent(rs.at[pl.ds(0, rows // 2)], PRE + i)
+        sent(rs.at[pl.ds(0, rows // 2)], ACT + i)
     sent(actp, ACTP)
     sent(shp, SHP)
     sent(shr.at[pl.ds(0, chips - 1)], SHARED)
@@ -419,6 +426,24 @@
     def _():
         sent(bk, BACK)
         sent(bk, DISP + first)
+
+
+def hand_over(*refs):
+    count = len(refs) // 2
+    sem = refs[-1]
+    copies = []
+    for n in range(count):
+        source, target = refs[n], refs[count + n]
+        if source.shape[0] == 2:
+            pairs = [(source.at[m], target.at[m]) for m in range(2)]
+        else:
+            pairs = [(source, target)]
+        for left, right in pairs:
+            copies.append(pltpu.make_async_copy(left, right, sem.at[len(copies)]))
+    for copy in copies:
+        copy.start()
+    for copy in copies:
+        copy.wait()
 
 
 def on_device(tokens, routes, gate_num, cotangent, w_in, w_out, shared_in, shared_out):
@@ -480,7 +505,14 @@
             collective_id=0, has_side_effects=True, vmem_limit_bytes=56 * 2**20
         ),
     )(tokens, cotangent, routes, gate_num, w_in[0], w_out[0], shared_in, shared_out)
-    out, gtok, gin, gout = results
+    out, gtok, gin, gout = pl.pallas_call(
+        hand_over,
+        out_shape=shapes,
+        in_specs=[hbm] * 4,
+        out_specs=(hbm,) * 4,
+        scratch_shapes=[pltpu.SemaphoreType.DMA((5,))],
+        compiler_params=pltpu.CompilerParams(vmem_limit_bytes=60 * 2**20),
+    )(*results)
     return out, gtok, gin[None], gout[None]
 
 

time: 152 us -> 224 us (1.47)
  the two profiles are of different devices: /device:TPU:33 before, /device:TPU:1 now
where the time goes in v3:
time: 224 us
  Pallas kernels  224 us (100%)
    pallas_call x1, Pallas kernels, on_device(): pl.pallas_call(functools.partial(kernel, topk), out_shape=shapes, in_spec...  128 us
    pallas_call x1, Pallas kernels, on_device(): pl.pallas_call(hand_over, out_shape=shapes, in_specs=[hbm] * 4, out_specs...  95.4 us

profile of v3, /device:TPU:1, one launch (start us, length us, event | category | flops | bytes accessed | tf_op | source)
XLA Modules:
  0.0 224.2 jit_solution(15098120677037732805)
XLA Ops:
  0.6 128.1 %shard_map.111 = (bf16[8,5120]{1,0:T(8,128)(2,1)}, bf16[8,5120]{1,0:T(8,128)(2,1)}, bf16[2,96,5120]{2,1,0:T(8,128)(2,1)}, bf16[96,5120]{1,0:T(8,128)(2,1)}) custom-call(bf16[8,5120]{1,0:T(8,128)(2,1)} %tok_ref.1, bf16[8,5120]{1,0:T(8,128)(2,1)} %cot_ref.1, s32[8,6]{1,0:T(8,128)} %routes_ref.1, s32[8,6]{1,0:T(8,128)} %gates_ref.1, ...), custom_call_target="tpu_custom_call" | custom-call | tf_op jit(solution)/shard_map/pallas_call | solution.py:498
  128.7 95.4 %shard_map.112 = (bf16[8,5120]{1,0:T(8,128)(2,1)}, bf16[8,5120]{1,0:T(8,128)(2,1)}, bf16[2,96,5120]{2,1,0:T(8,128)(2,1)}, bf16[96,5120]{1,0:T(8,128)(2,1)}) custom-call(bf16[8,5120]{1,0:T(8,128)(2,1)} %get-tuple-element.12.refs_0_, bf16[8,5120]{1,0:T(8,128)(2,1)} %get-tuple-element.13.refs_1_, bf16[2,96,5120]{2,1,0:T(8,128)(2,1)} %get-tuple-element.14.refs_2_, ...), custom_call_target="tpu_custom_call" | custom-call | tf_op jit(solution)/shard_map/pallas_call | solution.py:508

commit v4 on v3

--- a/solution.py
+++ b/solution.py
@@ -428,21 +428,24 @@
         sent(bk, DISP + first)
 
 
-def hand_over(*refs):
-    count = len(refs) // 2
-    sem = refs[-1]
-    copies = []
-    for n in range(count):
-        source, target = refs[n], refs[count + n]
-        if source.shape[0] == 2:
-            pairs = [(source.at[m], target.at[m]) for m in range(2)]
-        else:
-            pairs = [(source, target)]
-        for left, right in pairs:
-            copies.append(pltpu.make_async_copy(left, right, sem.at[len(copies)]))
-    for copy in copies:
+def hand_over(out_a, gtok_a, gin_a, gout_a, out_b, gtok_b, gin_b, gout_b, small, big, sem):
+    hid = gout_a.shape[0]
+    part = hid // 2
+    moves = []
+    for m in range(3):
+        left, right = (gout_a, gout_b) if m == 2 else (gin_a.at[m], gin_b.at[m])
+        for n in range(2):
+            rows = pl.ds(n * part, part)
+            moves.append((left.at[rows], big.at[m, rows], right.at[rows]))
+    moves += [(out_a, small.at[0], out_b), (gtok_a, small.at[1], gtok_b)]
+    inward = [pltpu.make_async_copy(src, mid, sem.at[0, n]) for n, (src, mid, _) in enumerate(moves)]
+    outward = [pltpu.make_async_copy(mid, dst, sem.at[1, n]) for n, (_, mid, dst) in enumerate(moves)]
+    for copy in inward:
         copy.start()
-    for copy in copies:
+    for before, after in zip(inward, outward):
+        before.wait()
+        after.start()
+    for copy in outward:
         copy.wait()
 
 
@@ -510,7 +513,11 @@
         out_shape=shapes,
         in_specs=[hbm] * 4,
         out_specs=(hbm,) * 4,
-        scratch_shapes=[pltpu.SemaphoreType.DMA((5,))],
+        scratch_shapes=[
+            pltpu.VMEM((2, own, features), BF),
+            pltpu.VMEM((3, hid, features), BF),
+            pltpu.SemaphoreType.DMA((2, 8)),
+        ],
         compiler_params=pltpu.CompilerParams(vmem_limit_bytes=60 * 2**20),
     )(*results)
     return out, gtok, gin[None], gout[None]

time: 224 us -> 132 us (0.59)
  Pallas kernels: 224 us -> 131 us
    pallas_call x1, Pallas kernels: 95.4 us -> 2.81 us  [on_device(): pl.pallas_call(hand_over, out_shape=shapes, in_specs=[hbm] * 4, out_specs...]
where the time goes in v4:
time: 132 us
  Pallas kernels  131 us (99%)
    pallas_call x1, Pallas kernels, on_device(): pl.pallas_call(functools.partial(kernel, topk), out_shape=shapes, in_spec...  128 us
    pallas_call x1, Pallas kernels, on_device(): pl.pallas_call(hand_over, out_shape=shapes, in_specs=[hbm] * 4, out_specs...  2.81 us

profile of v4, /device:TPU:1, one launch (start us, length us, event | category | flops | bytes accessed | tf_op | source)
XLA Modules:
  0.0 131.5 jit_solution(3414162420215054387)
XLA Ops:
  0.6 128.1 %shard_map.111 = (bf16[8,5120]{1,0:T(8,128)(2,1)}, bf16[8,5120]{1,0:T(8,128)(2,1)}, bf16[2,96,5120]{2,1,0:T(8,128)(2,1)}, bf16[96,5120]{1,0:T(8,128)(2,1)}) custom-call(bf16[8,5120]{1,0:T(8,128)(2,1)} %tok_ref.1, bf16[8,5120]{1,0:T(8,128)(2,1)} %cot_ref.1, s32[8,6]{1,0:T(8,128)} %routes_ref.1, s32[8,6]{1,0:T(8,128)} %gates_ref.1, ...), custom_call_target="tpu_custom_call" | custom-call | tf_op jit(solution)/shard_map/pallas_call | solution.py:501
  128.7 2.8 %shard_map.112 = (bf16[8,5120]{1,0:T(8,128)(2,1)}, bf16[8,5120]{1,0:T(8,128)(2,1)}, bf16[2,96,5120]{2,1,0:T(8,128)(2,1)}, bf16[96,5120]{1,0:T(8,128)(2,1)}) custom-call(bf16[8,5120]{1,0:T(8,128)(2,1)} %get-tuple-element.12.out_a, bf16[8,5120]{1,0:T(8,128)(2,1)} %get-tuple-element.13.gtok_a, bf16[2,96,5120]{2,1,0:T(8,128)(2,1)} %get-tuple-element.14.gin_a, ...), custom_call_target="tpu_custom_call" | custom-call | tf_op jit(solution)/shard_map/pallas_call | solution.py:511

commit v5 on v4

--- a/solution.py
+++ b/solution.py
@@ -15,8 +15,8 @@
 TN = (((0,), (0,)), ((), ()))
 
 TAB, SLICE, TOKX, TOKP, WPART, XP, ACTP, BACK, GRAD_IN, GRAD_OUT, SHP, SHARED, FINAL = range(13)
-PRE, ACT, WX, WF, DISP, PAIR, HALF = 13, 15, 17, 19, 21, 25, 29
-COUNT = 33
+PRE, ACT, WX, WF, DISP, PAIR, HALF = 13, 17, 21, 23, 25, 29, 33
+COUNT = 37
 
 
 def dot(left, right, dims=None):
@@ -54,7 +54,8 @@
     half = 4 * hid
     gl_count = ne // 2
     gq = gl_count // 4
-    rows = 2 * gq * SLOTS
+    rows = gq * SLOTS
+    own_rows = rows // 2
     m32 = 2 * SLOTS
 
     def rcopy(src, dst, which, dev):
@@ -182,8 +183,11 @@
             def _():
                 rcopy(from_here, target, DISP + first, (p, 2 * chip + (e // 4) % 2)).start()
 
+    def order(k):
+        return lax.rem(first + 4 - k, 4)
+
     def pass_rows(k):
-        chunk = lax.rem(first + 4 - k, 4)
+        chunk = order(k)
         part = xr.at[q, :, pl.ds(chunk * gq, gq)]
         recv(part, DISP + chunk)
         rcopy(part, part, PAIR + k, row_dev).start()
@@ -235,13 +239,12 @@
     pass_rows(2)
     shared_terms(nt // 2, nt)
     rcopy(shs.at[:, 1 - core], shp, SHP, (e, partner)).start()
-    pass_rows(3)
     pass_weights(1)
 
-    def products(quarter, n):
+    def products(quarter, chunk):
         value = [None] * 3
         for h in range(2):
-            part = xr[quarter, h, pl.ds(n * 2 * gq, 2 * gq)]
+            part = xr[quarter, h, pl.ds(chunk * gq, gq)]
             x_rows = part[:, :SLOTS].reshape(rows, d8)
             dy_rows = part[:, SLOTS:].reshape(rows, d8)
             for m in range(3):
@@ -249,75 +252,98 @@
                 value[m] = term if h == 0 else value[m] + term
         return value
 
+    def begin(k):
+        chunk = order(k)
+        for m, value in enumerate(products(q, chunk)):
+            pf[chunk, :, m * half:(m + 1) * half] = value
+
+    def finish(k):
+        chunk = order(k)
+        recv(xr.at[0, :, pl.ds(0, gq)], PAIR + k)
+        for m, value in enumerate(products(1 - q, chunk)):
+            span = slice(m * half, (m + 1) * half)
+            pf[chunk, :, span] = pf[chunk, :, span] + value
+        pb[chunk] = pf[chunk, block(1 - a, own_rows)].astype(BF)
+        rcopy(pb.at[chunk], rs.at[chunk], PRE + k, weight_dev).start()
+
+    def activate(k):
+        chunk = order(k)
+        recv(rs.at[chunk], PRE + k)
+        total = pf[chunk, block(a, own_rows)] + rs[chunk].astype(F32)
+        gate_pre, up_pre, back = total[:, :half], total[:, half:2 * half], total[:, 2 * half:]
+        active, slope = silu_parts(gate_pre)
+        act[chunk, a, :, :half] = (active * up_pre).astype(BF)
+        act[chunk, a, :, half:2 * half] = (back * up_pre * slope).astype(BF)
+        act[chunk, a, :, 2 * half:] = (back * active).astype(BF)
+        rcopy(act.at[chunk, a], act.at[chunk, a], ACT + k, weight_dev).start()
+
+    def results(quarter, h, chunk):
+        left = act[chunk].reshape(rows, 3 * half)
+        y = dot(left[:, :half], wt[quarter, h, 2])
+        dx = dot(left[:, half:], wt[quarter, h, 0:2].reshape(2 * half, d8))
+        return jnp.concatenate([y.reshape(gq, SLOTS, d8), dx.reshape(gq, SLOTS, d8)], axis=1)
+
+    def answer(k):
+        chunk = order(k)
+        part = pl.ds(chunk * gq, gq)
+        recv(act.at[chunk, 1 - a], ACT + k)
+        rcopy(act.at[chunk], actp.at[chunk], ACTP, (e, partner)).start()
+        for h in range(2):
+            ps[h, part] = results(1 - q, h, chunk).astype(BF)
+        rcopy(ps.at[:, part], pr.at[:, part], HALF + k, row_dev).start()
+        for h in range(2):
+            po[h, part] = results(q, h, chunk)
+
+    def give_back(k):
+        chunk = order(k)
+        part = pl.ds(chunk * gq, gq)
+        recv(pr.at[:, part], HALF + k)
+        ret[:, part] = (po[:, part] + pr[:, part].astype(F32)).astype(BF)
+
+        @pl.loop(0, gq)
+        def _(n):
+            place_here = chunk * gq + n
+            p = 4 * (2 * n + core) + chunk
+            for h in range(2):
+                local = jnp.logical_and(p == e, core == h)
+
+                @pl.when(local)
+                def _():
+                    pltpu.make_async_copy(ret.at[h, place_here], bk.at[home], rsem.at[BACK]).start()
+
+                @pl.when(jnp.logical_not(local))
+                def _():
+                    rcopy(ret.at[h, place_here], bk.at[home], BACK, (p, 2 * chip + h)).start()
+
     for copy in own_weights:
         copy.wait()
     recv(wt.at[:, :, :, pl.ds(0, hid)], WPART)
     recv(wt.at[0, :, :, pl.ds(0, hid)], WF)
-
-    @pl.loop(0, 2)
-    def _(n):
-        for m, value in enumerate(products(q, n)):
-            pf[n, :, m * half:(m + 1) * half] = value
-
+    for k in range(3):
+        begin(k)
     recv(shp, SHP)
     for n in range(chips):
         shs[n, core] = (shs[n, core].astype(F32) + shp[n].astype(F32)).astype(BF)
-
     for j in (weight_chip, lax.rem(chip + 2, chips)):
         rcopy(shs.at[j, core], shr.at[chip], SHARED, (e, 2 * j + core)).start()
     recv(wt.at[0, :, :, pl.ds(0, hid)], WF + 1)
-    for k in range(4):
-        recv(xr.at[0, :, pl.ds(0, gq)], PAIR + k)
-
-    def finish(n):
-        for m, value in enumerate(products(1 - q, n)):
-            span = slice(m * half, (m + 1) * half)
-            pf[n, :, span] = pf[n, :, span] + value
-
-    finish(1 - a)
-    pb[...] = pf[1 - a].astype(BF)
-    for i in range(2):
-        part = pl.ds(i * (rows // 2), rows // 2)
-        rcopy(pb.at[part], rs.at[part], PRE + i, weight_dev).start()
+    finish(0)
+    pass_rows(3)
+    activate(0)
+    begin(3)
+    finish(1)
+    answer(0)
+    activate(1)
+    finish(2)
+    answer(1)
+    activate(2)
+    finish(3)
     rcopy(xr.at[:, 1 - core], xp, XP, (e, partner)).start()
-
+    answer(2)
+    activate(3)
+    give_back(0)
+    answer(3)
     rcopy(shs.at[row_chip, core], shr.at[chip], SHARED, row_dev).start()
-    finish(a)
-    for i in range(2):
-        part = pl.ds(i * (rows // 2), rows // 2)
-        recv(rs.at[part], PRE + i)
-        total = pf[a, part] + rs[part].astype(F32)
-        gate_pre, up_pre, back = total[:, :half], total[:, half:2 * half], total[:, 2 * half:]
-        active, slope = silu_parts(gate_pre)
-        act[a, part, :half] = (active * up_pre).astype(BF)
-        act[a, part, half:2 * half] = (back * up_pre * slope).astype(BF)
-        act[a, part, 2 * half:] = (back * active).astype(BF)
-        rcopy(act.at[a, part], act.at[a, part], ACT + i, weight_dev).start()
-    for i in range(2):
-        recv(act.at[1 - a, pl.ds(i * (rows // 2), rows // 2)], ACT + i)
-    rcopy(act, actp, ACTP, (e, partner)).start()
-
-    def results(quarter, h, n):
-        y = dot(act[n, :, :half], wt[quarter, h, 2])
-        dx = dot(act[n, :, half:], wt[quarter, h, 0:2].reshape(2 * half, d8))
-        return jnp.concatenate([y.reshape(2 * gq, SLOTS, d8), dx.reshape(2 * gq, SLOTS, d8)], axis=1)
-
-    def order(k):
-        n = lax.rem(first // 2 + k // 2, 2)
-        return 2 * n + lax.rem(first + k, 2)
-
-    for k in range(2):
-        n = lax.rem(first // 2 + k, 2)
-        for h in range(2):
-            ps[h, pl.ds(n * 2 * gq, 2 * gq)] = results(1 - q, h, n).astype(BF)
-        for i in range(2):
-            part = pl.ds(order(2 * k + i) * gq, gq)
-            rcopy(ps.at[:, part], pr.at[:, part], HALF + 2 * k + i, row_dev).start()
-
-    @pl.loop(0, 2)
-    def _(n):
-        for h in range(2):
-            po[h, pl.ds(n * 2 * gq, 2 * gq)] = results(q, h, n)
 
     recv(xp, XP)
     recv(actp, ACTP)
@@ -326,10 +352,10 @@
     def gradient(n, m):
         span = slice(0, half) if m == 2 else slice((m + 1) * half, (m + 2) * half)
         kind = slice(SLOTS, m32) if m == 2 else slice(0, SLOTS)
-        here = act[:, :, span].reshape(2 * rows, half)
-        there = actp[:, :, span].reshape(2 * rows, half)
-        x_here = xr[n, core, :, kind].reshape(2 * rows, d8)
-        x_there = xp[n, :, kind].reshape(2 * rows, d8)
+        here = act[:, :, :, span].reshape(4 * rows, half)
+        there = actp[:, :, :, span].reshape(4 * rows, half)
+        x_here = xr[n, core, :, kind].reshape(4 * rows, d8)
+        x_there = xp[n, :, kind].reshape(4 * rows, d8)
         gb[n, m] = (dot(here, x_here, TN) + dot(there, x_there, TN)).astype(BF)
         target = (gout_ref if m == 2 else gin_ref.at[m]).at[:, cols(4 * a + 2 * n + core)]
         which = GRAD_OUT if m == 2 else GRAD_IN
@@ -340,34 +366,11 @@
         own.start()
         own_grads.append(own)
 
-    def give_back(k):
-        chunk = order(k)
-        part = pl.ds(chunk * gq, gq)
-        recv(pr.at[:, part], HALF + k)
-        ret[:, part] = (po[:, part] + pr[:, part].astype(F32)).astype(BF)
-
-        @pl.loop(0, gq)
-        def _(n):
-            place_here = chunk * gq + n
-            p = 4 * (2 * n + core) + chunk
-            for h in range(2):
-                local = jnp.logical_and(p == e, core == h)
-
-                @pl.when(local)
-                def _():
-                    pltpu.make_async_copy(ret.at[h, place_here], bk.at[home], rsem.at[BACK]).start()
-
-                @pl.when(jnp.logical_not(local))
-                def _():
-                    rcopy(ret.at[h, place_here], bk.at[home], BACK, (p, 2 * chip + h)).start()
-
     for m in range(3):
         gradient(0, m)
-    give_back(0)
-    gradient(1, 0)
-    gradient(1, 1)
     give_back(1)
-    gradient(1, 2)
+    for m in range(3):
+        gradient(1, m)
     give_back(2)
     give_back(3)
 
@@ -407,9 +410,9 @@
         sent(xr.at[0, :, pl.ds(0, gq)], PAIR + k)
         sent(ps.at[:, pl.ds(0, gq)], HALF + k)
     sent(xp, XP)
-    for i in range(2):
-        sent(rs.at[pl.ds(0, rows // 2)], PRE + i)
-        sent(rs.at[pl.ds(0, rows // 2)], ACT + i)
+    for k in range(4):
+        sent(rs.at[0], PRE + k)
+        sent(rs.at[0], ACT + k)
     sent(actp, ACTP)
     sent(shp, SHP)
     sent(shr.at[pl.ds(0, chips - 1)], SHARED)
@@ -456,7 +459,7 @@
     topk = routes.shape[1]
     hid, sh = w_out.shape[1], shared_out.shape[0]
     d8, half, gl_count = features // nt, 4 * hid, ne // 2
-    rows, m32 = gl_count * SLOTS // 2, 2 * SLOTS
+    rows, m32 = gl_count * SLOTS // 4, 2 * SLOTS
     vm = pl.BlockSpec(memory_space=pltpu.VMEM)
     hbm = pl.BlockSpec(memory_space=pl.ANY)
     scratch = [
@@ -472,11 +475,11 @@
         pltpu.VMEM((ne, m32, d8), BF),
         pltpu.VMEM((2, 2, gl_count, m32, d8), BF),
         pltpu.VMEM((2, gl_count, m32, d8), BF),
-        pltpu.VMEM((2, rows, 3 * half), F32),
-        pltpu.VMEM((rows, 3 * half), BF),
-        pltpu.VMEM((rows, 3 * half), BF),
-        pltpu.VMEM((2, rows, 3 * half), BF),
-        pltpu.VMEM((2, rows, 3 * half), BF),
+        pltpu.VMEM((4, rows, 3 * half), F32),
+        pltpu.VMEM((4, rows // 2, 3 * half), BF),
+        pltpu.VMEM((4, rows // 2, 3 * half), BF),
+        pltpu.VMEM((4, 2, rows // 2, 3 * half), BF),
+        pltpu.VMEM((4, 2, rows // 2, 3 * half), BF),
         pltpu.VMEM((2, gl_count, m32, d8), BF),
         pltpu.VMEM((2, gl_count, m32, d8), BF),
         pltpu.VMEM((2, gl_count, m32, d8), F32),

time: 132 us -> 135 us (1.023)
  Pallas kernels: 131 us -> 134 us
    pallas_call x1, Pallas kernels: 128 us -> 132 us  [on_device(): pl.pallas_call(functools.partial(kernel, topk), out_shape=shapes, in_spec...]
where the time goes in v5:
time: 135 us
  Pallas kernels  134 us (99%)
    pallas_call x1, Pallas kernels, on_device(): pl.pallas_call(functools.partial(kernel, topk), out_shape=shapes, in_spec...  132 us
    pallas_call x1, Pallas kernels, on_device(): pl.pallas_call(hand_over, out_shape=shapes, in_specs=[hbm] * 4, out_specs...  2.81 us

profile of v5, /device:TPU:1, one launch (start us, length us, event | category | flops | bytes accessed | tf_op | source)
XLA Modules:
  0.0 135.1 jit_solution(3340195564615027711)
XLA Ops:
  0.6 131.6 %shard_map.111 = (bf16[8,5120]{1,0:T(8,128)(2,1)}, bf16[8,5120]{1,0:T(8,128)(2,1)}, bf16[2,96,5120]{2,1,0:T(8,128)(2,1)}, bf16[96,5120]{1,0:T(8,128)(2,1)}) custom-call(bf16[8,5120]{1,0:T(8,128)(2,1)} %tok_ref.1, bf16[8,5120]{1,0:T(8,128)(2,1)} %cot_ref.1, s32[8,6]{1,0:T(8,128)} %routes_ref.1, s32[8,6]{1,0:T(8,128)} %gates_ref.1, ...), custom_call_target="tpu_custom_call" | custom-call | tf_op jit(solution)/shard_map/pallas_call | solution.py:504
  132.3 2.8 %shard_map.112 = (bf16[8,5120]{1,0:T(8,128)(2,1)}, bf16[8,5120]{1,0:T(8,128)(2,1)}, bf16[2,96,5120]{2,1,0:T(8,128)(2,1)}, bf16[96,5120]{1,0:T(8,128)(2,1)}) custom-call(bf16[8,5120]{1,0:T(8,128)(2,1)} %get-tuple-element.12.out_a, bf16[8,5120]{1,0:T(8,128)(2,1)} %get-tuple-element.13.gtok_a, bf16[2,96,5120]{2,1,0:T(8,128)(2,1)} %get-tuple-element.14.gin_a, ...), custom_call_target="tpu_custom_call" | custom-call | tf_op jit(solution)/shard_map/pallas_call | solution.py:514

commit v6 on v5

--- a/solution.py
+++ b/solution.py
@@ -119,11 +119,6 @@
         rcopy(table, tabs.at[block(t, 16)], TAB, (e, p)).start()
         rcopy(pair.at[:, cols(p)], gs.at[block(t, 16)], SLICE, (e, p)).start()
 
-    @pl.loop(1, chips)
-    def _(k):
-        rcopy(pair, g.at[block(t, 16)], TOKX, (e, lax.rem(t + 2 * k, nt))).start()
-
-    rcopy(pair, g.at[block(t, 16)], TOKP, (e, partner)).start()
     for n in range(2):
         there = n * q + (1 - n) * (1 - q)
         for h in range(2):
@@ -135,6 +130,8 @@
             for m in range(3):
                 rcopy(source(m).at[:, cols(4 * a + 2 * n + h)], wt.at[n, h, m, block(place, hid)],
                       WPART, (e, partner)).start()
+
+    rcopy(pair, g.at[block(t, 16)], TOKP, (e, partner)).start()
 
     tabs[block(t, 16), :] = table[...]
     gs[block(t, 16), :] = pair[:, cols(t)]
@@ -198,47 +195,10 @@
         recv(part, WX + n)
         rcopy(part, part, WF + n, (e, partner)).start()
 
-    recv(g.at[pl.ds(0, (chips - 1) * 16)], TOKX)
-
-    @pl.loop(1, chips)
-    def _(k):
-        part = g.at[block(lax.rem(t + 2 * k, nt), 16)]
-        rcopy(part, part, TOKP, (e, partner)).start()
-
     pass_rows(0)
-    recv(g.at[pl.ds(0, chips * 16)], TOKP)
-    for copy in own_shared:
-        copy.wait()
-    sh = sw_out.shape[0]
-
-    def shared_step(n, sums):
-        piece = g[:, cols(n)]
-        return tuple(
-            total + dot(piece, weight[:, cols(n)], NT)
-            for total, weight in zip(sums, (sw_in.at[0], sw_in.at[1], sw_out)))
-
-    zero = jnp.zeros((nt * 16, sh), F32)
-    sums = lax.fori_loop(0, nt, shared_step, (zero, zero, zero))
     pass_rows(1)
-    s_gate, s_up = [v.reshape(nt, 16, sh)[:, :8].reshape(nt * 8, sh) for v in sums[:2]]
-    s_back = sums[2].reshape(nt, 16, sh)[:, 8:].reshape(nt * 8, sh)
-    s_act, s_slope = silu_parts(s_gate)
-    s_hidden = (s_act * s_up).astype(BF)
-    s_dgate = (s_back * s_up * s_slope).astype(BF)
-    s_dup = (s_back * s_act).astype(BF)
-
-    def shared_terms(low, high):
-        @pl.loop(low, high)
-        def _(n):
-            y = dot(s_hidden, sw_out[:, cols(n)]).reshape(nt, 8, d8)
-            dx = (dot(s_dgate, sw_in[0, :, cols(n)]) + dot(s_dup, sw_in[1, :, cols(n)])).reshape(nt, 8, d8)
-            shs[:, :, :, cols(n)] = jnp.concatenate([y, dx], axis=1).astype(BF).reshape(chips, 2, 16, d8)
-
-    shared_terms(0, nt // 2)
     pass_weights(0)
     pass_rows(2)
-    shared_terms(nt // 2, nt)
-    rcopy(shs.at[:, 1 - core], shp, SHP, (e, partner)).start()
     pass_weights(1)
 
     def products(quarter, chunk):
@@ -321,13 +281,13 @@
     recv(wt.at[0, :, :, pl.ds(0, hid)], WF)
     for k in range(3):
         begin(k)
-    recv(shp, SHP)
-    for n in range(chips):
-        shs[n, core] = (shs[n, core].astype(F32) + shp[n].astype(F32)).astype(BF)
-    for j in (weight_chip, lax.rem(chip + 2, chips)):
-        rcopy(shs.at[j, core], shr.at[chip], SHARED, (e, 2 * j + core)).start()
     recv(wt.at[0, :, :, pl.ds(0, hid)], WF + 1)
     finish(0)
+
+    @pl.loop(1, chips)
+    def _(k):
+        rcopy(pair, g.at[block(t, 16)], TOKX, (e, lax.rem(t + 2 * k, nt))).start()
+
     pass_rows(3)
     activate(0)
     begin(3)
@@ -335,6 +295,14 @@
     answer(0)
     activate(1)
     finish(2)
+
+    recv(g.at[pl.ds(0, (chips - 1) * 16)], TOKX)
+
+    @pl.loop(1, chips)
+    def _(k):
+        part = g.at[block(lax.rem(t + 2 * k, nt), 16)]
+        rcopy(part, part, TOKP, (e, partner)).start()
+
     answer(1)
     activate(2)
     finish(3)
@@ -343,7 +311,6 @@
     activate(3)
     give_back(0)
     answer(3)
-    rcopy(shs.at[row_chip, core], shr.at[chip], SHARED, row_dev).start()
 
     recv(xp, XP)
     recv(actp, ACTP)
@@ -366,13 +333,52 @@
         own.start()
         own_grads.append(own)
 
+    give_back(1)
     for m in range(3):
         gradient(0, m)
-    give_back(1)
+    give_back(2)
     for m in range(3):
         gradient(1, m)
-    give_back(2)
     give_back(3)
+
+    recv(g.at[pl.ds(0, chips * 16)], TOKP)
+    for copy in own_shared:
+        copy.wait()
+    sh = sw_out.shape[0]
+
+    def shared_step(n, sums):
+        piece = g[:, cols(n)]
+        return tuple(
+            total + dot(piece, weight[:, cols(n)], NT)
+            for total, weight in zip(sums, (sw_in.at[0], sw_in.at[1], sw_out)))
+
+    zero = jnp.zeros((nt * 16, sh), F32)
+    sums = lax.fori_loop(0, nt, shared_step, (zero, zero, zero))
+    s_gate, s_up = [v.reshape(nt, 16, sh)[:, :8].reshape(nt * 8, sh) for v in sums[:2]]
+    s_back = sums[2].reshape(nt, 16, sh)[:, 8:].reshape(nt * 8, sh)
+    s_act, s_slope = silu_parts(s_gate)
+    s_hidden = (s_act * s_up).astype(BF)
+    s_dgate = (s_back * s_up * s_slope).astype(BF)
+    s_dup = (s_back * s_act).astype(BF)
+
+    def shared_terms(low, high):
+        @pl.loop(low, high)
+        def _(n):
+            y = dot(s_hidden, sw_out[:, cols(n)]).reshape(nt, 8, d8)
+            dx = (dot(s_dgate, sw_in[0, :, cols(n)]) + dot(s_dup, sw_in[1, :, cols(n)])).reshape(nt, 8, d8)
+            shs[:, :, :, cols(n)] = jnp.concatenate([y, dx], axis=1).astype(BF).reshape(chips, 2, 16, d8)
+
+    shared_terms(0, nt)
+    rcopy(shs.at[:, 1 - core], shp, SHP, (e, partner)).start()
+    recv(shp, SHP)
+    for n in range(chips):
+        shs[n, core] = (shs[n, core].astype(F32) + shp[n].astype(F32)).astype(BF)
+
+    @pl.loop(1, chips)
+    def _(k):
+        j = lax.rem(chip + k, chips)
+        rcopy(shs.at[j, core], shr.at[chip], SHARED, (e, 2 * j + core)).start()
+
 
     recv(bk, BACK)
     routed = dot(t2[...], bk[...].reshape(ne * m32, d8), TN)

time: 135 us -> 132 us (0.978)
  Pallas kernels: 134 us -> 132 us
    pallas_call x1, Pallas kernels: 132 us -> 129 us  [on_device(): pl.pallas_call(functools.partial(kernel, topk), out_shape=shapes, in_spec...]
where the time goes in v6:
time: 132 us
  Pallas kernels  132 us (100%)
    pallas_call x1, Pallas kernels, on_device(): pl.pallas_call(functools.partial(kernel, topk), out_shape=shapes, in_spec...  129 us
    pallas_call x1, Pallas kernels, on_device(): pl.pallas_call(hand_over, out_shape=shapes, in_specs=[hbm] * 4, out_specs...  2.81 us

profile of v6, /device:TPU:1, one launch (start us, length us, event | category | flops | bytes accessed | tf_op | source)
XLA Modules:
  0.0 132.3 jit_solution(1807214425427438793)
XLA Ops:
  0.6 128.7 %shard_map.111 = (bf16[8,5120]{1,0:T(8,128)(2,1)}, bf16[8,5120]{1,0:T(8,128)(2,1)}, bf16[2,96,5120]{2,1,0:T(8,128)(2,1)}, bf16[96,5120]{1,0:T(8,128)(2,1)}) custom-call(bf16[8,5120]{1,0:T(8,128)(2,1)} %tok_ref.1, bf16[8,5120]{1,0:T(8,128)(2,1)} %cot_ref.1, s32[8,6]{1,0:T(8,128)} %routes_ref.1, s32[8,6]{1,0:T(8,128)} %gates_ref.1, ...), custom_call_target="tpu_custom_call" | custom-call | tf_op jit(solution)/shard_map/pallas_call | solution.py:510
  129.4 2.8 %shard_map.112 = (bf16[8,5120]{1,0:T(8,128)(2,1)}, bf16[8,5120]{1,0:T(8,128)(2,1)}, bf16[2,96,5120]{2,1,0:T(8,128)(2,1)}, bf16[96,5120]{1,0:T(8,128)(2,1)}) custom-call(bf16[8,5120]{1,0:T(8,128)(2,1)} %get-tuple-element.12.out_a, bf16[8,5120]{1,0:T(8,128)(2,1)} %get-tuple-element.13.gtok_a, bf16[2,96,5120]{2,1,0:T(8,128)(2,1)} %get-tuple-element.14.gin_a, ...), custom_call_target="tpu_custom_call" | custom-call | tf_op jit(solution)/shard_map/pallas_call | solution.py:520

commit v7 on v6

--- a/solution.py
+++ b/solution.py
@@ -333,13 +333,10 @@
         own.start()
         own_grads.append(own)
 
+    for n in range(2):
+        for m in range(3):
+            gradient(n, m)
     give_back(1)
-    for m in range(3):
-        gradient(0, m)
-    give_back(2)
-    for m in range(3):
-        gradient(1, m)
-    give_back(3)
 
     recv(g.at[pl.ds(0, chips * 16)], TOKP)
     for copy in own_shared:
@@ -368,8 +365,10 @@
             dx = (dot(s_dgate, sw_in[0, :, cols(n)]) + dot(s_dup, sw_in[1, :, cols(n)])).reshape(nt, 8, d8)
             shs[:, :, :, cols(n)] = jnp.concatenate([y, dx], axis=1).astype(BF).reshape(chips, 2, 16, d8)
 
+    give_back(2)
     shared_terms(0, nt)
     rcopy(shs.at[:, 1 - core], shp, SHP, (e, partner)).start()
+    give_back(3)
     recv(shp, SHP)
     for n in range(chips):
         shs[n, core] = (shs[n, core].astype(F32) + shp[n].astype(F32)).astype(BF)

time: 132 us -> 132 us (level)
  no operation moved by 1% of the time
where the time goes in v7:
time: 132 us
  Pallas kernels  131 us (99%)
    pallas_call x1, Pallas kernels, on_device(): pl.pallas_call(functools.partial(kernel, topk), out_shape=shapes, in_spec...  129 us
    pallas_call x1, Pallas kernels, on_device(): pl.pallas_call(hand_over, out_shape=shapes, in_specs=[hbm] * 4, out_specs...  2.81 us

profile of v7, /device:TPU:1, one launch (start us, length us, event | category | flops | bytes accessed | tf_op | source)
XLA Modules:
  0.0 132.2 jit_solution(2385932661358870910)
XLA Ops:
  0.6 128.5 %shard_map.111 = (bf16[8,5120]{1,0:T(8,128)(2,1)}, bf16[8,5120]{1,0:T(8,128)(2,1)}, bf16[2,96,5120]{2,1,0:T(8,128)(2,1)}, bf16[96,5120]{1,0:T(8,128)(2,1)}) custom-call(bf16[8,5120]{1,0:T(8,128)(2,1)} %tok_ref.1, bf16[8,5120]{1,0:T(8,128)(2,1)} %cot_ref.1, s32[8,6]{1,0:T(8,128)} %routes_ref.1, s32[8,6]{1,0:T(8,128)} %gates_ref.1, ...), custom_call_target="tpu_custom_call" | custom-call | tf_op jit(solution)/shard_map/pallas_call | solution.py:509
  129.2 2.8 %shard_map.112 = (bf16[8,5120]{1,0:T(8,128)(2,1)}, bf16[8,5120]{1,0:T(8,128)(2,1)}, bf16[2,96,5120]{2,1,0:T(8,128)(2,1)}, bf16[96,5120]{1,0:T(8,128)(2,1)}) custom-call(bf16[8,5120]{1,0:T(8,128)(2,1)} %get-tuple-element.12.out_a, bf16[8,5120]{1,0:T(8,128)(2,1)} %get-tuple-element.13.gtok_a, bf16[2,96,5120]{2,1,0:T(8,128)(2,1)} %get-tuple-element.14.gin_a, ...), custom_call_target="tpu_custom_call" | custom-call | tf_op jit(solution)/shard_map/pallas_call | solution.py:519

commit v8 on v7

--- a/solution.py
+++ b/solution.py
@@ -16,7 +16,8 @@
 
 TAB, SLICE, TOKX, TOKP, WPART, XP, ACTP, BACK, GRAD_IN, GRAD_OUT, SHP, SHARED, FINAL = range(13)
 PRE, ACT, WX, WF, DISP, PAIR, HALF = 13, 17, 21, 23, 25, 29, 33
-COUNT = 37
+SUMS = 37
+COUNT = 38
 
 
 def dot(left, right, dims=None):
@@ -119,6 +120,7 @@
         rcopy(table, tabs.at[block(t, 16)], TAB, (e, p)).start()
         rcopy(pair.at[:, cols(p)], gs.at[block(t, 16)], SLICE, (e, p)).start()
 
+    rcopy(pair, g.at[block(t, 16)], TOKX, row_dev).start()
     for n in range(2):
         there = n * q + (1 - n) * (1 - q)
         for h in range(2):
@@ -284,10 +286,6 @@
     recv(wt.at[0, :, :, pl.ds(0, hid)], WF + 1)
     finish(0)
 
-    @pl.loop(1, chips)
-    def _(k):
-        rcopy(pair, g.at[block(t, 16)], TOKX, (e, lax.rem(t + 2 * k, nt))).start()
-
     pass_rows(3)
     activate(0)
     begin(3)
@@ -296,19 +294,14 @@
     activate(1)
     finish(2)
 
-    recv(g.at[pl.ds(0, (chips - 1) * 16)], TOKX)
-
-    @pl.loop(1, chips)
-    def _(k):
-        part = g.at[block(lax.rem(t + 2 * k, nt), 16)]
-        rcopy(part, part, TOKP, (e, partner)).start()
-
     answer(1)
     activate(2)
     finish(3)
     rcopy(xr.at[:, 1 - core], xp, XP, (e, partner)).start()
     answer(2)
     activate(3)
+    for j in (weight_chip, lax.rem(chip + 2, chips)):
+        rcopy(pair, g.at[block(t, 16)], TOKX, (e, 2 * j + core)).start()
     give_back(0)
     answer(3)
 
@@ -337,7 +330,14 @@
         for m in range(3):
             gradient(n, m)
     give_back(1)
-
+    recv(g.at[pl.ds(0, (chips - 1) * 16)], TOKX)
+
+    @pl.loop(1, chips)
+    def _(k):
+        part = g.at[block(lax.rem(t + 2 * k, nt), 16)]
+        rcopy(part, part, TOKP, (e, partner)).start()
+
+    give_back(2)
     recv(g.at[pl.ds(0, chips * 16)], TOKP)
     for copy in own_shared:
         copy.wait()
@@ -365,7 +365,6 @@
             dx = (dot(s_dgate, sw_in[0, :, cols(n)]) + dot(s_dup, sw_in[1, :, cols(n)])).reshape(nt, 8, d8)
             shs[:, :, :, cols(n)] = jnp.concatenate([y, dx], axis=1).astype(BF).reshape(chips, 2, 16, d8)
 
-    give_back(2)
     shared_terms(0, nt)
     rcopy(shs.at[:, 1 - core], shp, SHP, (e, partner)).start()
     give_back(3)
@@ -373,11 +372,12 @@
     for n in range(chips):
         shs[n, core] = (shs[n, core].astype(F32) + shp[n].astype(F32)).astype(BF)
 
-    @pl.loop(1, chips)
-    def _(k):
-        j = lax.rem(chip + k, chips)
-        rcopy(shs.at[j, core], shr.at[chip], SHARED, (e, 2 * j + core)).start()
-
+    rcopy(shs.at[row_chip, core], shr.at[0], SHARED, row_dev).start()
+    rcopy(shs.at[chips - 1 - row_chip, core], shr.at[1], SHARED, row_dev).start()
+    recv(shr.at[pl.ds(0, 2)], SHARED)
+    shs[weight_chip, core] = (shs[weight_chip, core].astype(F32) + shr[1].astype(F32)).astype(BF)
+    rcopy(shs.at[weight_chip, core], shr.at[2], SUMS, weight_dev).start()
+    shr[1] = shs[chip, core]
 
     recv(bk, BACK)
     routed = dot(t2[...], bk[...].reshape(ne * m32, d8), TN)
@@ -389,8 +389,7 @@
         rcopy(fs.at[p], fr.at[t], FINAL, (e, p)).start()
 
     fr[t] = fs[t]
-    shr[chip] = shs[chip, core]
-    recv(shr.at[pl.ds(0, chips - 1)], SHARED)
+    recv(shr.at[2], SUMS)
     recv(fr.at[pl.ds(0, nt - 1)], FINAL)
 
     for n in range(nt):
@@ -420,7 +419,8 @@
         sent(rs.at[0], ACT + k)
     sent(actp, ACTP)
     sent(shp, SHP)
-    sent(shr.at[pl.ds(0, chips - 1)], SHARED)
+    sent(shr.at[pl.ds(0, 2)], SHARED)
+    sent(shr.at[0], SUMS)
     sent(gin_ref.at[:, :, pl.ds(0, 6 * d8)], GRAD_IN)
     sent(gout_ref.at[:, pl.ds(0, 6 * d8)], GRAD_OUT)
     sent(fs.at[pl.ds(0, nt - 1)], FINAL)
@@ -493,7 +493,7 @@
         pltpu.VMEM((2, 3, half, d8), BF),
         pltpu.VMEM((chips, 2, 16, features), BF),
         pltpu.VMEM((chips, 16, features), BF),
-        pltpu.VMEM((chips, 16, features), BF),
+        pltpu.VMEM((3, 16, features), BF),
         pltpu.VMEM((nt, 16, d8), BF),
         pltpu.VMEM((nt, 16, d8), BF),
         pltpu.SemaphoreType.DMA((COUNT,)),

time: 132 us -> 129 us (0.977)
  Pallas kernels: 131 us -> 128 us
    pallas_call x1, Pallas kernels: 129 us -> 125 us  [on_device(): pl.pallas_call(functools.partial(kernel, topk), out_shape=shapes, in_spec...]
where the time goes in v8:
time: 129 us
  Pallas kernels  128 us (99%)
    pallas_call x1, Pallas kernels, on_device(): pl.pallas_call(functools.partial(kernel, topk), out_shape=shapes, in_spec...  125 us
    pallas_call x1, Pallas kernels, on_device(): pl.pallas_call(hand_over, out_shape=shapes, in_specs=[hbm] * 4, out_specs...  2.81 us

profile of v8, /device:TPU:1, one launch (start us, length us, event | category | flops | bytes accessed | tf_op | source)
XLA Modules:
  0.0 129.0 jit_solution(5620284969373635905)
XLA Ops:
  0.6 125.4 %shard_map.111 = (bf16[8,5120]{1,0:T(8,128)(2,1)}, bf16[8,5120]{1,0:T(8,128)(2,1)}, bf16[2,96,5120]{2,1,0:T(8,128)(2,1)}, bf16[96,5120]{1,0:T(8,128)(2,1)}) custom-call(bf16[8,5120]{1,0:T(8,128)(2,1)} %tok_ref.1, bf16[8,5120]{1,0:T(8,128)(2,1)} %cot_ref.1, s32[8,6]{1,0:T(8,128)} %routes_ref.1, s32[8,6]{1,0:T(8,128)} %gates_ref.1, ...), custom_call_target="tpu_custom_call" | custom-call | tf_op jit(solution)/shard_map/pallas_call | solution.py:509
  126.0 2.8 %shard_map.112 = (bf16[8,5120]{1,0:T(8,128)(2,1)}, bf16[8,5120]{1,0:T(8,128)(2,1)}, bf16[2,96,5120]{2,1,0:T(8,128)(2,1)}, bf16[96,5120]{1,0:T(8,128)(2,1)}) custom-call(bf16[8,5120]{1,0:T(8,128)(2,1)} %get-tuple-element.12.out_a, bf16[8,5120]{1,0:T(8,128)(2,1)} %get-tuple-element.13.gtok_a, bf16[2,96,5120]{2,1,0:T(8,128)(2,1)} %get-tuple-element.14.gin_a, ...), custom_call_target="tpu_custom_call" | custom-call | tf_op jit(solution)/shard_map/pallas_call | solution.py:519

commit v9 on v8

--- a/solution.py
+++ b/solution.py
@@ -201,7 +201,6 @@
     pass_rows(1)
     pass_weights(0)
     pass_rows(2)
-    pass_weights(1)
 
     def products(quarter, chunk):
         value = [None] * 3
@@ -283,6 +282,7 @@
     recv(wt.at[0, :, :, pl.ds(0, hid)], WF)
     for k in range(3):
         begin(k)
+    pass_weights(1)
     recv(wt.at[0, :, :, pl.ds(0, hid)], WF + 1)
     finish(0)
 
@@ -326,10 +326,11 @@
         own.start()
         own_grads.append(own)
 
-    for n in range(2):
-        for m in range(3):
-            gradient(n, m)
+    for m in range(3):
+        gradient(0, m)
     give_back(1)
+    for m in range(3):
+        gradient(1, m)
     recv(g.at[pl.ds(0, (chips - 1) * 16)], TOKX)
 
     @pl.loop(1, chips)

time: 129 us -> 128 us (level)
  no operation moved by 1% of the time
where the time goes in v9:
time: 128 us
  Pallas kernels  127 us (99%)
    pallas_call x1, Pallas kernels, on_device(): pl.pallas_call(functools.partial(kernel, topk), out_shape=shapes, in_spec...  125 us
    pallas_call x1, Pallas kernels, on_device(): pl.pallas_call(hand_over, out_shape=shapes, in_specs=[hbm] * 4, out_specs...  2.81 us

profile of v9, /device:TPU:1, one launch (start us, length us, event | category | flops | bytes accessed | tf_op | source)
XLA Modules:
  0.0 128.2 jit_solution(15351719843196178004)
XLA Ops:
  0.6 124.6 %shard_map.111 = (bf16[8,5120]{1,0:T(8,128)(2,1)}, bf16[8,5120]{1,0:T(8,128)(2,1)}, bf16[2,96,5120]{2,1,0:T(8,128)(2,1)}, bf16[96,5120]{1,0:T(8,128)(2,1)}) custom-call(bf16[8,5120]{1,0:T(8,128)(2,1)} %tok_ref.1, bf16[8,5120]{1,0:T(8,128)(2,1)} %cot_ref.1, s32[8,6]{1,0:T(8,128)} %routes_ref.1, s32[8,6]{1,0:T(8,128)} %gates_ref.1, ...), custom_call_target="tpu_custom_call" | custom-call | tf_op jit(solution)/shard_map/pallas_call | solution.py:510
  125.3 2.8 %shard_map.112 = (bf16[8,5120]{1,0:T(8,128)(2,1)}, bf16[8,5120]{1,0:T(8,128)(2,1)}, bf16[2,96,5120]{2,1,0:T(8,128)(2,1)}, bf16[96,5120]{1,0:T(8,128)(2,1)}) custom-call(bf16[8,5120]{1,0:T(8,128)(2,1)} %get-tuple-element.12.out_a, bf16[8,5120]{1,0:T(8,128)(2,1)} %get-tuple-element.13.gtok_a, bf16[2,96,5120]{2,1,0:T(8,128)(2,1)} %get-tuple-element.14.gin_a, ...), custom_call_target="tpu_custom_call" | custom-call | tf_op jit(solution)/shard_map/pallas_call | solution.py:520

commit v10 on v9

--- a/solution.py
+++ b/solution.py
@@ -283,12 +283,12 @@
     for k in range(3):
         begin(k)
     pass_weights(1)
+    pass_rows(3)
+    begin(3)
     recv(wt.at[0, :, :, pl.ds(0, hid)], WF + 1)
     finish(0)
 
-    pass_rows(3)
     activate(0)
-    begin(3)
     finish(1)
     answer(0)
     activate(1)

time: 128 us -> 128 us (level)
  no operation moved by 1% of the time
where the time goes in v10:
time: 128 us
  Pallas kernels  127 us (99%)
    pallas_call x1, Pallas kernels, on_device(): pl.pallas_call(functools.partial(kernel, topk), out_shape=shapes, in_spec...  124 us
    pallas_call x1, Pallas kernels, on_device(): pl.pallas_call(hand_over, out_shape=shapes, in_specs=[hbm] * 4, out_specs...  2.81 us

profile of v10, /device:TPU:1, one launch (start us, length us, event | category | flops | bytes accessed | tf_op | source)
XLA Modules:
  0.0 127.7 jit_solution(14416751511027476287)
XLA Ops:
  0.6 124.1 %shard_map.111 = (bf16[8,5120]{1,0:T(8,128)(2,1)}, bf16[8,5120]{1,0:T(8,128)(2,1)}, bf16[2,96,5120]{2,1,0:T(8,128)(2,1)}, bf16[96,5120]{1,0:T(8,128)(2,1)}) custom-call(bf16[8,5120]{1,0:T(8,128)(2,1)} %tok_ref.1, bf16[8,5120]{1,0:T(8,128)(2,1)} %cot_ref.1, s32[8,6]{1,0:T(8,128)} %routes_ref.1, s32[8,6]{1,0:T(8,128)} %gates_ref.1, ...), custom_call_target="tpu_custom_call" | custom-call | tf_op jit(solution)/shard_map/pallas_call | solution.py:510
  124.7 2.8 %shard_map.112 = (bf16[8,5120]{1,0:T(8,128)(2,1)}, bf16[8,5120]{1,0:T(8,128)(2,1)}, bf16[2,96,5120]{2,1,0:T(8,128)(2,1)}, bf16[96,5120]{1,0:T(8,128)(2,1)}) custom-call(bf16[8,5120]{1,0:T(8,128)(2,1)} %get-tuple-element.12.out_a, bf16[8,5120]{1,0:T(8,128)(2,1)} %get-tuple-element.13.gtok_a, bf16[2,96,5120]{2,1,0:T(8,128)(2,1)} %get-tuple-element.14.gin_a, ...), custom_call_target="tpu_custom_call" | custom-call | tf_op jit(solution)/shard_map/pallas_call | solution.py:520
